TPU v7x, 32 devices: a whole 2x2x4 slice. The times are simulated.
32 devices in a mesh: dp: 8 (over z, y), pipe: 4 (over x, core).
Axes of the slice: x: 2, y: 2, z: 4, core: 2. Of those that a mesh axis runs over, the one named last changes fastest.
Arguments:
- series_input: float32 [2, 180, 256, 128], P(None, None, 'dp'), may hold values from -6 to 6
- cotangent: float32 [2, 180, 256, 128], P(None, None, 'dp'), may hold values from -6 to 6
- season_enter_first: bfloat16 [2, 48, 96], replicated, may hold values from -0.625 to 0.625
- season_enter_second: bfloat16 [2, 24, 48], replicated, may hold values from -0.875 to 0.875
- season_enter_third: bfloat16 [2, 12, 24], replicated, may hold values from -1.25 to 1.25
- season_leave_first: bfloat16 [2, 48, 48], replicated, may hold values from -0.875 to 0.875
- season_leave_second: bfloat16 [2, 24, 24], replicated, may hold values from -1.25 to 1.25
- season_leave_third: bfloat16 [2, 12, 12], replicated, may hold values from -1.75 to 1.75
- season_bias: bfloat16 [2, 2, 84], replicated, may hold values from -3 to 3
- trend_enter_first: bfloat16 [2, 96, 48], replicated, may hold values from -0.875 to 0.875
- trend_enter_second: bfloat16 [2, 48, 24], replicated, may hold values from -1.25 to 1.25
- trend_enter_third: bfloat16 [2, 24, 12], replicated, may hold values from -1.75 to 1.75
- trend_leave_first: bfloat16 [2, 96, 96], replicated, may hold values from -0.625 to 0.625
- trend_leave_second: bfloat16 [2, 48, 48], replicated, may hold values from -0.875 to 0.875
- trend_leave_third: bfloat16 [2, 24, 24], replicated, may hold values from -1.25 to 1.25
- trend_bias: bfloat16 [2, 2, 168], replicated, may hold values from -3 to 3
- expand_weight: bfloat16 [2, 128, 256], replicated, may hold values from -0.5 to 0.5
- expand_bias: bfloat16 [2, 256], replicated, may hold values from -3 to 3
- shrink_weight: bfloat16 [2, 256, 128], replicated, may hold values from -0.375 to 0.375
- shrink_bias: bfloat16 [2, 128], replicated, may hold values from -3 to 3
- norm_gain: bfloat16 [2, 4, 128], replicated, may hold values from 0.5 to 1.5
- norm_shift: bfloat16 [2, 4, 128], replicated, may hold values from -3 to 3
Outputs:
- layer_output: float32 [2, 180, 256, 128], P(None, None, 'dp')
- input_grad: float32 [2, 180, 256, 128], P(None, None, 'dp')
- grad_season_enter_first: float32 [2, 48, 96], replicated
- grad_season_enter_second: float32 [2, 24, 48], replicated
- grad_season_enter_third: float32 [2, 12, 24], replicated
- grad_season_leave_first: float32 [2, 48, 48], replicated
- grad_season_leave_second: float32 [2, 24, 24], replicated
- grad_season_leave_third: float32 [2, 12, 12], replicated
- grad_season_bias: float32 [2, 2, 84], replicated
- grad_trend_enter_first: float32 [2, 96, 48], replicated
- grad_trend_enter_second: float32 [2, 48, 24], replicated
- grad_trend_enter_third: float32 [2, 24, 12], replicated
- grad_trend_leave_first: float32 [2, 96, 96], replicated
- grad_trend_leave_second: float32 [2, 48, 48], replicated
- grad_trend_leave_third: float32 [2, 24, 24], replicated
- grad_trend_bias: float32 [2, 2, 168], replicated
- grad_expand_weight: float32 [2, 128, 256], replicated
- grad_expand_bias: float32 [2, 256], replicated
- grad_shrink_weight: float32 [2, 256, 128], replicated
- grad_shrink_bias: float32 [2, 128], replicated
- grad_norm_gain: float32 [2, 4, 128], replicated
- grad_norm_shift: float32 [2, 4, 128], replicated
All inputs are finite; a program needn't handle non-finite values.
Results may differ from a plain program's by a relative error of at most 0.022.
Values may be sent and summed in bfloat16 or wider, within the bound.
No kernel may reach another device: no remote copies, remote signals or barrier semaphores. Data moves between devices by JAX's collectives and lax.ppermute only.
A program may use at most 192 MiB of HBM per device.

v0:
```python
import jax
import jax.numpy as jnp
from jax import lax
from jax.sharding import PartitionSpec as P

L0 = 96
KERNEL = 25


EPSILON = 1e-05
PRECISE = lax.Precision.HIGHEST


def passed_along(block, axis, distance):
    devices = range(lax.axis_size(axis))
    route = [(i - distance, i) for i in devices if i - distance in devices]
    return lax.ppermute(block, axis, route)


def for_sending(value):
    return jax.tree.map(lambda a: a.astype(jnp.bfloat16) if a.dtype == jnp.float32 else a, value)


def average_matrix(length):
    row_index = jnp.arange(length)[:, None]
    reached = jnp.clip(row_index + jnp.arange(KERNEL)[None, :] - KERNEL // 2, 0, length - 1)
    matches = (reached[:, :, None] == jnp.arange(length)[None, None, :]).astype(jnp.float32)
    return jnp.sum(matches, axis=1) / KERNEL


def scale_layout():
    lengths = [L0 // 2**scale_at for scale_at in range(4)]
    starts = [sum(lengths[:scale_at]) for scale_at in range(4)]
    return (lengths, starts)


def contract_last(left_side, right_side):
    return lax.dot_general(
        left_side, right_side, (((1,), (1,)), ((), ())), preferred_element_type=jnp.float32
    )


def contract_first(left_side, right_side):
    return lax.dot_general(
        left_side, right_side, (((0,), (0,)), ((), ())), preferred_element_type=jnp.float32
    )


def normalize(residual, gain_row, shift_row):
    average = jnp.mean(residual, axis=-1, keepdims=True)
    centred = residual - average
    spread = jnp.mean(centred * centred, axis=-1, keepdims=True)
    return centred * lax.rsqrt(spread + EPSILON) * gain_row + shift_row


def time_forward(source, enter_weight, enter_bias, leave_weight, leave_bias):
    source_low = source.astype(jnp.bfloat16)
    before = (
        jnp.dot(enter_weight, source_low, preferred_element_type=jnp.float32)
        + enter_bias.astype(jnp.float32)[:, None]
    )
    active_low = jax.nn.gelu(before).astype(jnp.bfloat16)
    result = (
        jnp.dot(leave_weight, active_low, preferred_element_type=jnp.float32)
        + leave_bias.astype(jnp.float32)[:, None]
    )
    return (result, (source_low, before, active_low))


def time_backward(upstream, enter_weight, leave_weight, stored):
    source_low, before, active_low = stored
    upstream_low = upstream.astype(jnp.bfloat16)
    grad_leave_bias = jnp.sum(upstream_low, axis=1, dtype=jnp.float32)
    grad_leave = contract_last(upstream_low, active_low)
    grad_active = contract_first(leave_weight, upstream_low)
    _, gelu_pull = jax.vjp(jax.nn.gelu, before)
    before_low = gelu_pull(grad_active)[0].astype(jnp.bfloat16)
    grad_enter_bias = jnp.sum(before_low, axis=1, dtype=jnp.float32)
    grad_enter = contract_last(before_low, source_low)
    grad_source = contract_first(enter_weight, before_low)
    return (grad_source, (grad_enter, grad_enter_bias, grad_leave, grad_leave_bias))


def layer_forward(block_in, weights):
    lengths, starts = scale_layout()
    season_enter = weights[0:3]
    season_leave = weights[3:6]
    season_bias = weights[6]
    trend_enter = weights[7:10]
    trend_leave = weights[10:13]
    trend_bias = weights[13]
    expand_weight, expand_bias, shrink_weight, shrink_bias, norm_gain, norm_shift = weights[14:20]
    features = expand_weight.shape[0]
    pieces = [
        block_in[starts[scale_at] : starts[scale_at] + lengths[scale_at]] for scale_at in range(4)
    ]
    trends = [
        jnp.dot(average_matrix(lengths[scale_at]), pieces[scale_at], precision=PRECISE)
        for scale_at in range(4)
    ]
    seasons = [pieces[scale_at] - trends[scale_at] for scale_at in range(4)]
    mixed_season = [seasons[0]]
    season_kept = []
    for scale_at in range(3):
        offset = starts[scale_at + 1] - lengths[0]
        span_len = lengths[scale_at + 1]
        mixed_in, stored = time_forward(
            mixed_season[scale_at],
            season_enter[scale_at],
            season_bias[0, offset : offset + span_len],
            season_leave[scale_at],
            season_bias[1, offset : offset + span_len],
        )
        mixed_season.append(seasons[scale_at + 1] + mixed_in)
        season_kept.append(stored)
    mixed_trend = [None, None, None, trends[3]]
    trend_kept = [None, None, None]
    for scale_at in (2, 1, 0):
        offset = starts[scale_at]
        span_len = lengths[scale_at]
        mixed_in, stored = time_forward(
            mixed_trend[scale_at + 1],
            trend_enter[scale_at],
            trend_bias[0, offset : offset + span_len],
            trend_leave[scale_at],
            trend_bias[1, offset : offset + span_len],
        )
        mixed_trend[scale_at] = trends[scale_at] + mixed_in
        trend_kept[scale_at] = stored
    outputs = []
    branch_kept = []
    for scale_at in range(4):
        joined_low = (
            (mixed_season[scale_at] + mixed_trend[scale_at])
            .reshape(-1, features)
            .astype(jnp.bfloat16)
        )
        hidden = jnp.dot(
            joined_low, expand_weight, preferred_element_type=jnp.float32
        ) + expand_bias.astype(jnp.float32)
        active_low = jax.nn.gelu(hidden).astype(jnp.bfloat16)
        branch = jnp.dot(
            active_low, shrink_weight, preferred_element_type=jnp.float32
        ) + shrink_bias.astype(jnp.float32)
        residual = pieces[scale_at].reshape(-1, features) + branch
        normed, norm_pull = jax.vjp(
            normalize,
            residual,
            norm_gain[scale_at].astype(jnp.float32),
            norm_shift[scale_at].astype(jnp.float32),
        )
        outputs.append(normed.reshape(lengths[scale_at], -1))
        branch_kept.append((joined_low, hidden, active_low, norm_pull))
    return (jnp.concatenate(outputs, axis=0), (season_kept, trend_kept, branch_kept))


def layer_backward(kept_state, upstream, weights):
    season_kept, trend_kept, branch_kept = kept_state
    lengths, starts = scale_layout()
    season_enter = weights[0:3]
    season_leave = weights[3:6]
    trend_enter = weights[7:10]
    trend_leave = weights[10:13]
    expand_weight = weights[14]
    shrink_weight = weights[16]
    features = expand_weight.shape[0]
    grad_joined = []
    grad_residual = []
    grad_gain = []
    grad_shift = []
    grad_expand = 0.0
    grad_expand_bias = 0.0
    grad_shrink = 0.0
    grad_shrink_bias = 0.0
    for scale_at in range(4):
        joined_low, hidden, active_low, norm_pull = branch_kept[scale_at]
        rows_up = upstream[starts[scale_at] : starts[scale_at] + lengths[scale_at]].reshape(
            -1, features
        )
        back_residual, back_gain, back_shift = norm_pull(rows_up)
        residual_low = back_residual.astype(jnp.bfloat16)
        grad_shrink_bias = grad_shrink_bias + jnp.sum(residual_low, axis=0, dtype=jnp.float32)
        grad_shrink = grad_shrink + contract_first(active_low, residual_low)
        back_active = contract_last(residual_low, shrink_weight)
        _, gelu_pull = jax.vjp(jax.nn.gelu, hidden)
        hidden_low = gelu_pull(back_active)[0].astype(jnp.bfloat16)
        grad_expand_bias = grad_expand_bias + jnp.sum(hidden_low, axis=0, dtype=jnp.float32)
        grad_expand = grad_expand + contract_first(joined_low, hidden_low)
        back_joined = contract_last(hidden_low, expand_weight)
        grad_joined.append(back_joined.reshape(lengths[scale_at], -1))
        grad_residual.append(back_residual.reshape(lengths[scale_at], -1))
        grad_gain.append(back_gain)
        grad_shift.append(back_shift)
    back_season = [None, None, None, grad_joined[3]]
    season_grads = [None, None, None]
    for scale_at in (2, 1, 0):
        back_source, season_grads[scale_at] = time_backward(
            back_season[scale_at + 1],
            season_enter[scale_at],
            season_leave[scale_at],
            season_kept[scale_at],
        )
        back_season[scale_at] = grad_joined[scale_at] + back_source
    back_trend = [grad_joined[0], None, None, None]
    trend_grads = [None, None, None]
    for scale_at in range(3):
        back_source, trend_grads[scale_at] = time_backward(
            back_trend[scale_at], trend_enter[scale_at], trend_leave[scale_at], trend_kept[scale_at]
        )
        back_trend[scale_at + 1] = grad_joined[scale_at + 1] + back_source
    back_pieces = []
    for scale_at in range(4):
        matrix = average_matrix(lengths[scale_at])
        averaged = lax.dot_general(
            matrix,
            back_trend[scale_at] - back_season[scale_at],
            (((0,), (0,)), ((), ())),
            precision=PRECISE,
            preferred_element_type=jnp.float32,
        )
        back_pieces.append(grad_residual[scale_at] + back_season[scale_at] + averaged)
    back_block = jnp.concatenate(back_pieces, axis=0)
    season_bias_grad = jnp.stack(
        [
            jnp.concatenate([season_grads[scale_at][1] for scale_at in range(3)]),
            jnp.concatenate([season_grads[scale_at][3] for scale_at in range(3)]),
        ]
    )
    trend_bias_grad = jnp.stack(
        [
            jnp.concatenate([trend_grads[scale_at][1] for scale_at in range(3)]),
            jnp.concatenate([trend_grads[scale_at][3] for scale_at in range(3)]),
        ]
    )
    grads = (
        season_grads[0][0],
        season_grads[1][0],
        season_grads[2][0],
        season_grads[0][2],
        season_grads[1][2],
        season_grads[2][2],
        season_bias_grad,
        trend_grads[0][0],
        trend_grads[1][0],
        trend_grads[2][0],
        trend_grads[0][2],
        trend_grads[1][2],
        trend_grads[2][2],
        trend_bias_grad,
        grad_expand,
        grad_expand_bias,
        grad_shrink,
        grad_shrink_bias,
        jnp.stack(grad_gain),
        jnp.stack(grad_shift),
    )
    return (back_block, grads)


def run_sections(series_input, cotangent, weights):
    pipe_size = lax.axis_size("pipe")
    section_size = pipe_size // 2
    position = lax.axis_index("pipe")
    section_at = position // section_size
    inner_at = position % section_size
    micro_count, time_rows, local_series, features = series_input.shape
    per_device = local_series // section_size
    own_input = lax.dynamic_slice_in_dim(series_input, inner_at * per_device, per_device, 2)
    own_input = own_input.reshape(micro_count, time_rows, per_device * features)
    own_tangent = lax.dynamic_slice_in_dim(cotangent, inner_at * per_device, per_device, 2)
    own_tangent = own_tangent.reshape(micro_count, time_rows, per_device * features)
    chosen = tuple(
        (
            lax.dynamic_index_in_dim(weight_in, section_at, 0, keepdims=False)
            for weight_in in weights
        )
    )
    leading = section_at == 0
    received = jnp.zeros((time_rows, per_device * features), jnp.bfloat16)
    stored_inputs = []
    results = []
    for tick_at in range(micro_count + 1):
        current = jnp.where(
            leading, own_input[min(tick_at, micro_count - 1)], received.astype(jnp.float32)
        )
        result, _ = layer_forward(current, chosen)
        if tick_at >= 1:
            stored_inputs.append(received)
            results.append(result)
        if tick_at < micro_count:
            received = passed_along(result.astype(jnp.bfloat16), "pipe", section_size)
    back_received = jnp.zeros((time_rows, per_device * features), jnp.float32)
    running = tuple((jnp.zeros(weight_in.shape, jnp.float32) for weight_in in chosen))
    back_list = []
    for tick_at in range(micro_count + 1):
        later = min(tick_at, micro_count - 1)
        earlier = max(tick_at - 1, 0)
        current = jnp.where(leading, own_input[earlier], stored_inputs[later].astype(jnp.float32))
        incoming = jnp.where(leading, back_received, own_tangent[later])
        _, kept_state = layer_forward(current, chosen)
        back_block, grads = layer_backward(kept_state, incoming, chosen)
        weight_on = jnp.where(
            leading, 1.0 if tick_at >= 1 else 0.0, 1.0 if tick_at < micro_count else 0.0
        )
        running = tuple((so_far + weight_on * update for so_far, update in zip(running, grads)))
        if tick_at >= 1:
            back_list.append(back_block)
        if tick_at < micro_count:
            back_received = passed_along(
                back_block.astype(jnp.bfloat16), "pipe", -section_size
            ).astype(jnp.float32)
    own_piece = jnp.where(leading, jnp.stack(back_list), jnp.stack(results))
    own_piece = own_piece.reshape(micro_count, time_rows, per_device, features)
    gathered = lax.all_gather(own_piece.astype(jnp.bfloat16), "pipe", axis=2, tiled=True).astype(
        own_piece.dtype
    )
    input_grad = gathered[:, :, :local_series]
    layer_output = gathered[:, :, local_series:]
    summed = lax.psum(running, "dp")
    own_slot = leading.astype(jnp.float32)
    stacked = tuple(
        (jnp.stack([update * own_slot, update * (1.0 - own_slot)]) for update in summed)
    )
    totals = jax.tree.map(
        lambda part: part.astype(jnp.float32), lax.psum(for_sending(stacked), "pipe")
    )
    return (layer_output, input_grad) + tuple(totals)


def shards(
    series_input,
    cotangent,
    season_enter_first,
    season_enter_second,
    season_enter_third,
    season_leave_first,
    season_leave_second,
    season_leave_third,
    season_bias,
    trend_enter_first,
    trend_enter_second,
    trend_enter_third,
    trend_leave_first,
    trend_leave_second,
    trend_leave_third,
    trend_bias,
    expand_weight,
    expand_bias,
    shrink_weight,
    shrink_bias,
    norm_gain,
    norm_shift,
):
    weights = (
        season_enter_first,
        season_enter_second,
        season_enter_third,
        season_leave_first,
        season_leave_second,
        season_leave_third,
        season_bias,
        trend_enter_first,
        trend_enter_second,
        trend_enter_third,
        trend_leave_first,
        trend_leave_second,
        trend_leave_third,
        trend_bias,
        expand_weight,
        expand_bias,
        shrink_weight,
        shrink_bias,
        norm_gain,
        norm_shift,
    )
    return run_sections(series_input, cotangent, weights)


def solution(mesh):
    return jax.shard_map(
        shards,
        mesh=mesh,
        in_specs=(
            P(None, None, "dp", None),
            P(None, None, "dp", None),
            P(),
            P(),
            P(),
            P(),
            P(),
            P(),
            P(),
            P(),
            P(),
            P(),
            P(),
            P(),
            P(),
            P(),
            P(),
            P(),
            P(),
            P(),
            P(),
            P(),
        ),
        out_specs=(
            P(None, None, "dp", None),
            P(None, None, "dp", None),
            P(),
            P(),
            P(),
            P(),
            P(),
            P(),
            P(),
            P(),
            P(),
            P(),
            P(),
            P(),
            P(),
            P(),
            P(),
            P(),
            P(),
            P(),
            P(),
            P(),
        ),
        check_vma=False,
    )
```

profile of v0, /device:TPU:0, one launch (start us, length us, event | category | flops | bytes accessed | tf_op | source)
XLA Modules:
  0.0 919.8 jit_solution(17715109552734164270)
XLA Ops:
  12.9 2.1 dynamic-slice_bitcast_fusion.2
  35.4 2.4 fusion.18
  37.8 2.7 fusion.13
  42.5 2.5 add_convert_fusion.6
  45.8 2.5 fusion.1236
  48.3 2.0 add_convert_fusion.12
  55.6 2.3 copy.177
  57.9 2.2 fusion.1239
  62.7 2.1 dynamic-slice_select_fusion
  69.4 2.0 pad_maximum_fusion.2
  71.4 6.1 collective-permute-start
  80.1 12.6 %collective-permute-done = bf16[180,2048]{1,0:T(8,128)(2,1)} collective-permute-done((bf16[180,2048]{1,0:T(8,128)(2,1)}, bf16[180,2048]{1,0:T(8,128)(2,1)}, u32[]{:S(2)}, u32[]{:S(2)}) %collective-permute-start) | collective-permute-done | bytes 737312 | tf_op jit(solution)/shard_map/ppermute | solution.py:17
  97.4 2.0 fusion.27
  99.4 2.4 fusion.21
  101.8 2.3 add_convert_fusion.3
  104.1 2.4 fusion.15
  112.4 2.1 add_convert_fusion.9
  125.5 5.5 collective-permute-start.2
  138.4 7.0 collective-permute-done.2
  145.4 3.0 convert_select_fusion.3
  190.8 2.3 convert_reduce_fusion.62
  211.6 2.4 convert_reduce_fusion.56
  221.0 2.4 convert_reduce_fusion.53
  236.0 2.8 convert_reduce_fusion.9
  242.4 2.0 convert_reduce_fusion.33
  244.4 2.0 convolution_multiply_fusion.7
  254.8 2.1 reshape.1091
  257.0 2.3 copy.185
  265.1 2.7 convert_reduce_fusion.2
  267.8 2.3 copy.186
  270.2 2.3 fusion.1250
  278.3 2.7 convert_reduce_fusion.15
  297.4 2.4 copy.187
  299.7 2.2 reshape.1093
  302.0 2.5 convolution_multiply_fusion.1
  341.2 2.4 fusion.1220
  346.7 2.2 reshape.1115
  348.9 2.3 copy.205
  352.4 2.2 add_convert_fusion.2
  375.9 2.3 reshape.1131
  378.2 2.4 copy.217
  413.3 11.3 %collective-permute-done.1 = bf16[180,2048]{1,0:T(8,128)(2,1)S(1)} collective-permute-done((bf16[180,2048]{1,0:T(8,128)(2,1)S(1)}, bf16[180,2048]{1,0:T(8,128)(2,1)S(1)}, u32[]{:S(2)}, u32[]{:S(2)}) %collective-permute-start.1) | collective-permute-done | bytes 737312 | tf_op jit(solution)/shard_map/ppermute | solution.py:17
  438.6 2.6 convert_reduce_fusion.21
  456.8 2.7 convert_reduce_fusion.1
  459.5 2.4 copy.206
  467.5 3.4 convert_reduce_fusion.8
  471.9 2.0 convert_reduce_fusion.12
  482.2 2.5 convert_reduce_fusion.51
  488.5 2.0 fusion.652
  494.3 2.9 convert_reduce_fusion.32
  501.7 3.0 convert_reduce_fusion.13
  530.5 9.4 %collective-permute-done.3 = bf16[180,2048]{1,0:T(8,128)(2,1)S(1)} collective-permute-done((bf16[180,2048]{1,0:T(8,128)(2,1)S(1)}, bf16[180,2048]{1,0:T(8,128)(2,1)S(1)}, u32[]{:S(2)}, u32[]{:S(2)}) %collective-permute-start.3) | collective-permute-done | bytes 737312 | tf_op jit(solution)/shard_map/ppermute | solution.py:17
  570.5 2.0 convert_reduce_fusion.7
  582.9 2.1 fusion.640
  596.2 2.1 convert_reduce_fusion.30
  599.8 2.1 convert_reduce_fusion.24
  601.9 2.4 convolution_add_fusion.26
  620.5 2.2 fusion.97
  631.6 76.7 %all-reduce.9.cloned.1.call-done = (f32[12,24]{1,0:T(8,128)}, f32[12,12]{1,0:T(8,128)}, f32[24,12]{0,1:T(8,128)}, f32[48,96]{1,0:T(8,128)}, f32[24,48]{1,0:T(8,1...) async-done(((f32[12,24]{1,0:T(8,128)}, f32[12,12]{1,0:T(8,128)}, ...) | async-done | bytes 116528 | tf_op jit(solution)/shard_map/psum | solution.py:319
  731.8 51.2 %all-reduce.11.cloned.1.call-done = (f32[128,256]{1,0:T(8,128)}, f32[256,128]{1,0:T(8,128)}) async-done(((f32[128,256]{1,0:T(8,128)}, f32[256,128]{1,0:T(8,128)}), (f32[128,256]{1,0:T(8,128)}, f32[256,128]{1,0:T(8,128)})) %all-reduce.11.cloned.1.call-update) | async-done | bytes 262160 | tf_op jit(solution)/shard_map/psum | solution.py:319
  787.7 32.8 %all-reduce.13.cloned.1.call-done = (bf16[2,12,24]{2,1,0:T(8,128)(2,1)}, bf16[2,12,12]{2,1,0:T(8,128)(2,1)}, bf16[2,24,12]{1,2,0:T(8,128)(2,1)}, bf16[2,48,96]{2...) async-done(((bf16[2,12,24]{2,1,0:T(8,128)(2,1)}, ...) | async-done | bytes 116528 | tf_op jit(solution)/shard_map/psum | solution.py:325
  844.1 13.1 %all-reduce.15.cloned.1.call-done = (bf16[2,128,256]{2,1,0:T(8,128)(2,1)}, bf16[2,256,128]{2,1,0:T(8,128)(2,1)}) async-done(((bf16[2,128,256]{2,1,0:T(8,128)(2,1)}, bf16[2,256,128]{2,1,0:T(8,128)(2,1)}), (bf16[2,128,256]{2,1,0:T(8,128)(2,1)}, bf16[2,256,128]{2,1,0:T(8,128)(2,1)})) %all-reduce.15.cloned.1.call-update) | async-done | bytes 262160 | tf_op jit(solution)/shard_map/psum | solution.py:325
  860.4 43.7 %all-gather.2.cloned.1.call-done = bf16[2,180,64,128]{3,2,1,0:T(8,128)(2,1)} async-done(((bf16[2,180,16,128]{3,2,1,0:T(8,128)(2,1)}), bf16[2,180,64,128]{3,2,1,0:T(8,128)(2,1)}) %all-gather.2.cloned.1.call-update) | async-done | bytes 5898256 | tf_op jit(solution)/shard_map/all_gather | solution.py:314
  904.1 9.0 fusion.1218
  (1716 shorter events, 498.5 us)
Async XLA Ops:
  7.2 38.6 %copy-start = (bf16[2,128,256]{2,1,0:T(8,128)(2,1)S(1)}, bf16[2,128,256]{2,1,0:T(8,128)(2,1)}, u32[]{:S(2)}) copy-start(bf16[2,128,256]{2,1,0:T(8,128)(2,1)} %param.38) | copy-start | bytes 393220
  7.2 701.1 %all-reduce.9.cloned.1.call-start = ((), (), s32[]{:S(2)}) async-start(), calls=%async_computation.1 | async-start | bytes 459776 | tf_op jit(solution)/shard_map/psum | solution.py:319
  15.9 34.5 %copy-start.4 = (f32[180,2048]{1,0:T(8,128)}, f32[180,2048]{1,0:T(8,128)S(1)}, u32[]{:S(2)}) copy-start(f32[180,2048]{1,0:T(8,128)S(1)} %broadcast_select_fusion) | copy-start | bytes 4423684
  19.9 95.5 %copy-start.267 = (bf16[1,12,24]{2,1,0:T(8,128)(2,1)}, bf16[1,12,24]{2,1,0:T(8,128)(2,1)S(1)}, u32[]{:S(2)}) copy-start(bf16[1,12,24]{2,1,0:T(8,128)(2,1)S(1)} %copy.264) | copy-start | bytes 1732
  20.6 76.8 %copy-start.270 = (bf16[1,24,12]{1,2,0:T(8,128)(2,1)}, bf16[1,24,12]{1,2,0:T(8,128)(2,1)S(1)}, u32[]{:S(2)}) copy-start(bf16[1,24,12]{1,2,0:T(8,128)(2,1)S(1)} %copy.266) | copy-start | bytes 1732
  20.7 130.6 %copy-start.213 = (f32[12,12]{1,0:T(8,128)}, f32[12,12]{1,0:T(8,128)S(1)}, u32[]{:S(2)}) copy-start(f32[12,12]{1,0:T(8,128)S(1)} %convert_reduce_fusion.63) | copy-start | bytes 1732
  20.8 74.0 %copy-start.155 = (f32[24,24]{1,0:T(8,128)}, f32[24,24]{1,0:T(8,128)S(1)}, u32[]{:S(2)}) copy-start(f32[24,24]{1,0:T(8,128)S(1)} %convert_reduce_fusion.35) | copy-start | bytes 6916
  21.1 138.5 %copy-start.77 = (f32[48,48]{1,0:T(8,128)}, f32[48,48]{1,0:T(8,128)S(1)}, u32[]{:S(2)}) copy-start(f32[48,48]{1,0:T(8,128)S(1)} %convert_reduce_fusion.16) | copy-start | bytes 27652
  21.6 141.6 %copy-start.32 = (f32[96,96]{1,0:T(8,128)}, f32[96,96]{1,0:T(8,128)S(1)}, u32[]{:S(2)}) copy-start(f32[96,96]{1,0:T(8,128)S(1)} %convert_reduce_fusion.3) | copy-start | bytes 110596
  53.1 7.0 copy-start.251
  71.4 21.2 %collective-permute-start = (bf16[180,2048]{1,0:T(8,128)(2,1)}, bf16[180,2048]{1,0:T(8,128)(2,1)}, u32[]{:S(2)}, u32[]{:S(2)}) collective-permute-start(bf16[180,2048]{1,0:T(8,128)(2,1)} %pad_maximum_fusion.2), channel_id=1, source_target_pairs={{0,2},{1,3},{4,6},{5,7},{8,10},{9,11},{12,14},{13,15},{16,18},{17,... | collective-permute-start | bytes 2211848 | tf_op jit(solution)/shard_map/ppermute | solution.py:17
  78.2 14.4 %copy-start.7 = (f32[23,8,16,128]{3,1,2,0:T(8,128)}, f32[23,8,16,128]{3,1,2,0:T(8,128)S(1)}, u32[]{:S(2)}) copy-start(f32[23,8,16,128]{3,1,2,0:T(8,128)S(1)} %copy.258) | copy-start | bytes 4521988
  124.2 6.8 copy-start.31
  125.5 19.9 %collective-permute-start.2 = (bf16[180,2048]{1,0:T(8,128)(2,1)}, bf16[180,2048]{1,0:T(8,128)(2,1)}, u32[]{:S(2)}, u32[]{:S(2)}) collective-permute-start(bf16[180,2048]{1,0:T(8,128)(2,1)} %pad_maximum_fusion.4), channel_id=1, source_target_pairs={{0,2},{1,3},{4,6},{5,7},{8,10},{9,11},{12,14},{13,15},{16,18},{17,... | collective-permute-start | bytes 2211848 | tf_op jit(solution)/shard_map/ppermute | solution.py:17
  148.4 14.8 %copy-start.1 = (f32[180,2048]{1,0:T(8,128)}, f32[180,2048]{1,0:T(8,128)S(1)}, u32[]{:S(2)}) copy-start(f32[180,2048]{1,0:T(8,128)S(1)} %get-tuple-element.264) | copy-start | bytes 4423684
  148.7 17.7 %copy-start.148 = (f32[12,2048]{1,0:T(8,128)}, f32[12,2048]{1,0:T(8,128)S(1)}, u32[]{:S(2)}) copy-start(f32[12,2048]{1,0:T(8,128)S(1)} %fusion.939) | copy-start | bytes 294916
  153.1 14.2 %copy-start.98 = (f32[24,2048]{1,0:T(8,128)}, f32[24,2048]{1,0:T(8,128)S(1)}, u32[]{:S(2)}) copy-start(f32[24,2048]{1,0:T(8,128)S(1)} %fusion.856) | copy-start | bytes 589828
  193.1 7.4 copy-start.321
  203.1 8.6 copy-start.442
  223.5 6.7 copy-start.518
  286.4 9.2 copy-start.48
  305.7 12.6 %copy-start.94 = (f32[24,2048]{1,0:T(8,128)S(1)}, f32[24,2048]{1,0:T(8,128)}, u32[]{:S(2)}) copy-start(f32[24,2048]{1,0:T(8,128)} %fusion.848) | copy-start | bytes 589828
  309.7 11.4 %copy-start.97 = (f32[24,2048]{1,0:T(8,128)S(1)}, f32[24,2048]{1,0:T(8,128)}, u32[]{:S(2)}) copy-start(f32[24,2048]{1,0:T(8,128)} %fusion.851) | copy-start | bytes 589828
  313.2 10.3 %copy-start.313 = (bf16[2,48,24]{1,2,0:T(8,128)(2,1)S(1)}, bf16[2,48,24]{1,2,0:T(8,128)(2,1)}, u32[]{:S(2)}) copy-start(bf16[2,48,24]{1,2,0:T(8,128)(2,1)} %param.32) | copy-start | bytes 13828
  324.5 7.5 copy-start.37
  324.5 7.5 copy-start.409
  335.7 16.7 %copy-start.19 = (f32[48,2048]{1,0:T(8,128)}, f32[48,2048]{1,0:T(8,128)S(1)}, u32[]{:S(2)}) copy-start(f32[48,2048]{1,0:T(8,128)S(1)} %fusion.22) | copy-start | bytes 1179652
  354.6 8.2 copy-start.153
  355.7 15.7 %copy-start.90 = (bf16[768,128]{1,0:T(8,128)(2,1)}, bf16[768,128]{1,0:T(8,128)(2,1)S(1)}, u32[]{:S(2)}) copy-start(bf16[768,128]{1,0:T(8,128)(2,1)S(1)} %convert_element_type.1443) | copy-start | bytes 589828
  363.7 7.7 copy-start.289
  364.6 7.0 copy-start.284
  365.8 6.9 copy-start.519
  375.9 19.4 %copy-start.35 = (bf16[1536,128]{1,0:T(8,128)(2,1)}, bf16[1536,128]{1,0:T(8,128)(2,1)S(1)}, u32[]{:S(2)}) copy-start(bf16[1536,128]{1,0:T(8,128)(2,1)S(1)} %convert_element_type.1484) | copy-start | bytes 1179652
  383.0 8.4 copy-start.92
  383.5 6.6 copy-start.160
  405.8 18.8 %collective-permute-start.1 = (bf16[180,2048]{1,0:T(8,128)(2,1)S(1)}, bf16[180,2048]{1,0:T(8,128)(2,1)S(1)}, u32[]{:S(2)}, u32[]{:S(2)}) collective-permute-start(bf16[180,2048]{1,0:T(8,128)(2,1)S(1)} %pad_maximum_fusion.3), channel_id=1, source_target_pairs={{2,0},{3,1},{6,4},{7,5},{10,8},{11,9},{14,12},{15,13},{18,16},{19,... | collective-permute-start | bytes 2211848 | tf_op jit(solution)/shard_map/ppermute | solution.py:17
  412.2 12.4 %copy-start.6 = (f32[23,8,16,128]{3,1,2,0:T(8,128)S(1)}, f32[23,8,16,128]{3,1,2,0:T(8,128)}, u32[]{:S(2)}) copy-start(f32[23,8,16,128]{3,1,2,0:T(8,128)} %copy.257) | copy-start | bytes 4521988
  427.6 6.6 slice-start.1
  476.9 8.7 copy-start.51
  522.0 17.9 %collective-permute-start.3 = (bf16[180,2048]{1,0:T(8,128)(2,1)S(1)}, bf16[180,2048]{1,0:T(8,128)(2,1)S(1)}, u32[]{:S(2)}, u32[]{:S(2)}) collective-permute-start(bf16[180,2048]{1,0:T(8,128)(2,1)S(1)} %pad_maximum_fusion), channel_id=1, source_target_pairs={{2,0},{3,1},{6,4},{7,5},{10,8},{11,9},{14,12},{15,13},{18,16},{19,... | collective-permute-start | bytes 2211848 | tf_op jit(solution)/shard_map/ppermute | solution.py:17
  530.4 10.8 %copy-start.359 = (f32[128]{0:T(128)S(1)}, f32[128]{0:T(128)}, u32[]{:S(2)}) copy-start(f32[128]{0:T(128)} %get-tuple-element.334) | copy-start | bytes 1540
  530.4 10.8 %copy-start.375 = (f32[192]{0:T(256)S(1)}, f32[192]{0:T(256)}, u32[]{:S(2)}) copy-start(f32[192]{0:T(256)} %copy-done.374) | copy-start | bytes 2308
  530.4 10.8 %copy-start.393 = (f32[192]{0:T(256)S(1)}, f32[192]{0:T(256)}, u32[]{:S(2)}) copy-start(f32[192]{0:T(256)} %copy-done.392) | copy-start | bytes 2308
  530.4 11.6 %copy-start.396 = (f32[192]{0:T(256)S(1)}, f32[192]{0:T(256)}, u32[]{:S(2)}) copy-start(f32[192]{0:T(256)} %copy-done.395) | copy-start | bytes 2308
  530.4 12.5 %copy-start.283 = (f32[192,256]{1,0:T(8,128)S(1)}, f32[192,256]{1,0:T(8,128)}, u32[]{:S(2)}) copy-start(f32[192,256]{1,0:T(8,128)} %copy-done.282) | copy-start | bytes 589828
  530.4 12.5 %copy-start.511 = (bf16[2,256,128]{2,1,0:T(8,128)(2,1)S(1)}, bf16[2,256,128]{2,1,0:T(8,128)(2,1)}, u32[]{:S(2)}) copy-start(bf16[2,256,128]{2,1,0:T(8,128)(2,1)} %param.40) | copy-start | bytes 393220
  582.9 7.0 copy-start.63
  582.9 7.0 copy-start.308
  620.4 10.4 %copy-start.324 = (f32[128]{0:T(128)S(1)}, f32[128]{0:T(128)}, u32[]{:S(2)}) copy-start(f32[128]{0:T(128)} %get-tuple-element.335) | copy-start | bytes 1540
  620.4 10.4 %copy-start.349 = (f32[384]{0:T(512)S(1)}, f32[384]{0:T(512)}, u32[]{:S(2)}) copy-start(f32[384]{0:T(512)} %broadcast_multiply_fusion.10) | copy-start | bytes 4612
  620.5 10.4 %copy-start.361 = (f32[384]{0:T(512)S(1)}, f32[384]{0:T(512)}, u32[]{:S(2)}) copy-start(f32[384]{0:T(512)} %copy-done.360) | copy-start | bytes 4612
  620.5 10.4 %copy-start.420 = (f32[128]{0:T(128)S(1)}, f32[128]{0:T(128)}, u32[]{:S(2)}) copy-start(f32[128]{0:T(128)} %get-tuple-element.339) | copy-start | bytes 1540
  622.7 8.4 copy-start.188
  622.7 8.5 copy-start.123
  630.8 152.2 %all-reduce.11.cloned.1.call-start = ((), (), s32[]{:S(2)}) async-start(), calls=%async_computation.2 | async-start | bytes 524288 | tf_op jit(solution)/shard_map/psum | solution.py:319
  631.5 154.8 %copy-start.76 = (bf16[1,180,16,128]{3,2,1,0:T(8,128)(2,1)S(1)}, bf16[1,180,16,128]{3,2,1,0:T(8,128)(2,1)}, u32[]{:S(2)}) copy-start(bf16[1,180,16,128]{3,2,1,0:T(8,128)(2,1)} %slice_bitcast_fusion.1) | copy-start | bytes 2211844
  631.5 154.8 %copy-start.100 = (bf16[1536,128]{1,0:T(8,128)(2,1)S(1)}, bf16[1536,128]{1,0:T(8,128)(2,1)}, u32[]{:S(2)}) copy-start(bf16[1536,128]{1,0:T(8,128)(2,1)} %copy.229) | copy-start | bytes 1179652
  631.5 154.8 %copy-start.169 = (bf16[768,128]{1,0:T(8,128)(2,1)S(1)}, bf16[768,128]{1,0:T(8,128)(2,1)}, u32[]{:S(2)}) copy-start(bf16[768,128]{1,0:T(8,128)(2,1)} %copy.230) | copy-start | bytes 589828
  631.5 154.8 %copy-start.231 = (bf16[192,128]{1,0:T(8,128)(2,1)S(1)}, bf16[192,128]{1,0:T(8,128)(2,1)}, u32[]{:S(2)}) copy-start(bf16[192,128]{1,0:T(8,128)(2,1)} %copy-done.230) | copy-start | bytes 147460
  631.5 154.8 %copy-start.257 = (bf16[384,128]{1,0:T(8,128)(2,1)S(1)}, bf16[384,128]{1,0:T(8,128)(2,1)}, u32[]{:S(2)}) copy-start(bf16[384,128]{1,0:T(8,128)(2,1)} %copy.231) | copy-start | bytes 294916
  631.6 154.8 %copy-start.278 = (bf16[192,128]{1,0:T(8,128)(2,1)S(1)}, bf16[192,128]{1,0:T(8,128)(2,1)}, u32[]{:S(2)}) copy-start(bf16[192,128]{1,0:T(8,128)(2,1)} %multiply_add_fusion.6) | copy-start | bytes 147460
  631.6 189.0 %all-reduce.13.cloned.1.call-start = ((), (), s32[]{:S(2)}) async-start(), calls=%async_computation.3 | async-start | bytes 459776 | tf_op jit(solution)/shard_map/psum | solution.py:325
  731.8 125.4 %all-reduce.15.cloned.1.call-start = ((), (), s32[]{:S(2)}) async-start(), calls=%async_computation.4 | async-start | bytes 524288 | tf_op jit(solution)/shard_map/psum | solution.py:325
  786.2 117.9 %all-gather.2.cloned.1.call-start = ((), (), s32[]{:S(2)}) async-start(), calls=%async_computation | async-start | bytes 7372800 | tf_op jit(solution)/shard_map/all_gather | solution.py:314
  (488 other events, 1525.6 us)
Sparse Core Ops, SparseCore 0:
  630.9 77.3 all-reduce.8
  712.8 70.1 all-reduce.10
  788.5 32.0 all-reduce.12
  823.5 33.5 all-reduce.14
  859.1 44.9 all-gather.1
where the time goes:
time: 934 us; the launch traced here: 920 us
  matrix products  292 us (31%)
  waiting for transfers between devices  258 us (28%)
  local copies, waits for them, and re-layouts  200 us (21%)
  other arithmetic  134 us (14%)
  between operations  20.2 us (2%)
  starting transfers between devices  14.7 us (2%)
    psum x2, waiting for transfers between devices, run_sections(): summed = lax.psum(running, 'dp')  128 us
    dot_general x60, matrix products, contract_first(): lax.dot_general(left_side, right_side, (((0,), (0,)), ((), ())), preferre...  83.8 us
    dot_general x60, matrix products, contract_last(): lax.dot_general(left_side, right_side, (((1,), (1,)), ((), ())), preferre...  82.4 us
    reshape x35, local copies, waits for them, and re-layouts, layer_forward(): residual = pieces[scale_at].reshape(-1, features) + branch  54.1 us
    psum x2, waiting for transfers between devices, run_sections(): lax.psum(for_sending(stacked), 'pipe')  45.9 us
    dot_general x30, matrix products, time_forward(): jnp.dot(leave_weight, active_low, preferred_element_type=jnp.float32)  43.9 us
    all_gather x1, waiting for transfers between devices, run_sections(): lax.all_gather(own_piece.astype(jnp.bfloat16), 'pipe', axis=2, tiled=True)  43.7 us
    ppermute x4, waiting for transfers between devices, passed_along(): return lax.ppermute(block, axis, route)  40.3 us
  transfers between devices with their start and end apart: 9, of which 9 were waited for; matrix products, arithmetic and copies ran while one was open for 8% of the time, Pallas kernels for 0%

commit v1 on v0

v1 whole, which is shorter than its diff:
```python
import functools

import jax
import jax.numpy as jnp
import numpy as np
from jax import lax
from jax.experimental import pallas as pl
from jax.experimental.pallas import tpu as pltpu
from jax.sharding import PartitionSpec as P

F32 = jnp.float32
BF16 = jnp.bfloat16

LENGTHS = (96, 48, 24, 12)
STARTS = (0, 96, 144, 168)
STEPS = 180
ROWS = 192
KERNEL = 25
LAYERS = 2
WIDTH = 128
HIDDEN = 256
GROUP = 8
EPSILON = 1e-05

ROWS_OF = {96: 96, 48: 48, 24: 24, 12: 16}
AUG = {96: 112, 48: 64, 24: 32, 12: 16}
DEEP = {96: 96, 48: 48, 24: 32, 12: 16}

FROM = (96, 48, 24, 12, 24, 48)
TO = (48, 24, 12, 24, 48, 96)
BIAS_AT = (0, 48, 72, 144, 96, 0)
ENTER_ARG = (0, 1, 2, 9, 8, 7)
LEAVE_ARG = (3, 4, 5, 12, 11, 10)
BIAS_ARG = (6, 6, 6, 13, 13, 13)

ORDER = {2: (1, 0, 2), 5: (1, 0, 2), 7: (0, 2, 1), 8: (0, 2, 1), 9: (2, 0, 1)}
MIDDLE = (2, 5, 9)
TURNED = (7, 8, 9)


def offsets(sizes):
    total, found = 0, []
    for size in sizes:
        found.append(total)
        total += size
    return found, total


SOURCE_AT, SOURCE_ROWS = offsets([AUG[n] for n in FROM])
ACTIVE_AT, ACTIVE_ROWS = offsets([AUG[n] for n in TO])
SLOPE_AT, SLOPE_ROWS = offsets([ROWS_OF[n] for n in TO])
FROM_AT, FROM_ROWS = offsets([DEEP[n] for n in FROM])
TO_AT, TO_ROWS = offsets([DEEP[n] for n in TO])

PIECES = ((0, 48, 0), (48, 96, 0), (96, 144, 1), (144, 168, 2), (168, 192, 3))

VECTORS_AT = 288
EXPAND_AT = 304
SHRINK_AT = 560
USED_ROWS = 816

GELU_A = 0.7978845608028654
GELU_B = GELU_A * 0.044715


def dot(left, right):
    return lax.dot_general(left, right, (((1,), (0,)), ((), ())), preferred_element_type=F32)


def dot_last(left, right):
    return lax.dot_general(left, right, (((1,), (1,)), ((), ())), preferred_element_type=F32)


def dot_first(left, right):
    return lax.dot_general(left, right, (((0,), (0,)), ((), ())), preferred_element_type=F32)


def gelu_and_slope(u):
    square = u * u
    half = jnp.tanh(u * (GELU_A + GELU_B * square)) * 0.5 + 0.5
    value = u * half
    slope = half + (value - value * half) * (2.0 * GELU_A + 6.0 * GELU_B * square)
    return value, slope


def iota(shape, dim):
    return lax.broadcasted_iota(jnp.int32, shape, dim)


def eye(rows, lanes):
    return (iota((rows, lanes), 0) == iota((rows, lanes), 1)).astype(F32)


def moving_average():
    total = np.zeros((ROWS, ROWS), np.float32)
    for start, length in zip(STARTS, LENGTHS):
        for row in range(length):
            for offset in range(KERNEL):
                reached = min(max(row + offset - KERNEL // 2, 0), length - 1)
                total[start + row, start + reached] += 1.0
    return total


def prepare(weights, keep):
    keep.means[...] = keep.counts[...].astype(BF16)
    keep.stage[...] = jnp.zeros(keep.stage.shape, F32)
    unit = eye(WIDTH, WIDTH).astype(BF16)
    for layer in range(LAYERS):
        for block in range(6):
            rows, cols = TO[block], FROM[block]
            full = DEEP[rows]
            enter_back = keep.enter_back.at[layer, FROM_AT[block] : FROM_AT[block] + DEEP[cols]]
            near = slice(TO_AT[block], TO_AT[block] + full)
            leave_back = keep.leave_back.at[layer, near]
            for arg, depth, place, straight, back in (
                (ENTER_ARG[block], cols, 0, keep.enter.at[layer, near], enter_back),
                (LEAVE_ARG[block], rows, 1, keep.leave.at[layer, near], leave_back),
            ):
                stage = keep.stage.at[layer, block, place]
                if arg in MIDDLE:
                    value = weights[arg][...].astype(F32)[:, layer, :]
                else:
                    value = weights[arg][layer].astype(F32)
                stage[0 : value.shape[0], 0 : value.shape[1]] = value
                if arg in TURNED:
                    turned = dot_last(unit, stage[...].astype(BF16))
                    stage[:, 0:96] = turned[0:96]
                    stage[:, 96:] = jnp.zeros((96, WIDTH - 96), F32)
                matrix = stage[0:full, :]
                source = weights[BIAS_ARG[block]][layer, place : place + 1, :].astype(F32)
                at = BIAS_AT[block]
                lanes = source.shape[1]
                pick = iota((full, lanes), 1) - at == iota((full, lanes), 0)
                pick = pick & (iota((full, lanes), 0) < rows)
                column = jnp.sum(jnp.where(pick, source, 0.0), axis=1, keepdims=True)
                here = jnp.where(iota((full, WIDTH), 1) == depth, column, matrix)
                straight[...] = here.astype(BF16)
                turned = dot_last(unit, matrix.astype(BF16))
                back[:, 0:full] = turned[0 : DEEP[depth]].astype(BF16)
        expand, shrink = weights[14][layer], weights[16][layer]
        keep.expand_back[layer] = dot_last(eye(HIDDEN, HIDDEN).astype(BF16), expand).astype(BF16)
        keep.shrink_back[layer] = dot_last(unit, shrink).astype(BF16)


def rows_in(start, stop, size):
    return [(at, min(at + size, stop)) for at in range(start, stop, size)]


def store_with_ones(ref, value, length):
    for at, end in rows_in(0, length, 16):
        piece = value[at : min(at + 16, value.shape[0])]
        if length == 12:
            row = iota(piece.shape, 0)
            piece = jnp.where(row < 12, piece, jnp.where(row == 12, 1.0, 0.0))
        elif end - at < 16:
            tail = (iota((8, piece.shape[1]), 0) == 0).astype(F32)
            piece = jnp.concatenate([piece, tail], axis=0)
        ref[at : at + 16, :] = piece.astype(BF16)


def padded(value, length):
    if length == 24:
        return jnp.concatenate([value, jnp.zeros((8, value.shape[1]), F32)], axis=0).astype(BF16)
    return value.astype(BF16)


def scale_rows(scale):
    return STARTS[scale], STARTS[scale] + ROWS_OF[LENGTHS[scale]]


def time_forward(layer, keep, lanes):
    if layer == 0:
        mean = keep.means[0]
        trend = dot(mean, keep.split[0:ROWS, lanes]) + dot(mean, keep.split[ROWS:, lanes])
    else:
        trend = dot(keep.means[0], keep.second_in[:, lanes])
    season_ref, trend_ref = keep.season, keep.trend
    source_ref, active_ref = keep.source, keep.active
    for at, end in rows_in(0, ROWS, 16):
        average = trend[at:end] * (1.0 / KERNEL)
        if layer == 0:
            value = keep.first_in[at:end, lanes]
        else:
            value = keep.second_in[at:end, lanes].astype(F32)
        trend_ref[at:end, lanes] = average
        season_ref[at:end, lanes] = value - average
    yield

    def block_forward(block, value_ref, from_scale, to_scale):
        into, to = FROM[block], TO[block]
        rows = ROWS_OF[to]
        at, end = scale_rows(from_scale)
        source = source_ref.at[layer, SOURCE_AT[block] : SOURCE_AT[block] + AUG[into], lanes]
        store_with_ones(source, value_ref[at:end, lanes], into)
        before = dot(
            keep.enter[layer, TO_AT[block] : TO_AT[block] + rows, 0 : AUG[into]], source[...]
        )
        yield
        active = active_ref.at[layer, ACTIVE_AT[block] : ACTIVE_AT[block] + AUG[to], lanes]
        for at, end in rows_in(0, rows, 16):
            value, slope = gelu_and_slope(before[at:end])
            keep.slope[layer, SLOPE_AT[block] + at : SLOPE_AT[block] + end, lanes] = slope
            if to >= 48:
                active[at:end, :] = value.astype(BF16)
            elif to == 24:
                if end - at < 16:
                    tail = (iota((8, value.shape[1]), 0) == 0).astype(F32)
                    value = jnp.concatenate([value, tail], axis=0)
                active[at : at + 16, :] = value.astype(BF16)
            else:
                store_with_ones(active, value, to)
        out = dot(keep.leave[layer, TO_AT[block] : TO_AT[block] + rows, 0 : AUG[to]], active[...])
        yield
        start, _ = scale_rows(to_scale)
        for at, end in rows_in(0, rows, 16):
            value_ref[start + at : start + end, lanes] += out[at:end]

    for step in range(3):
        pair = [
            block_forward(step, season_ref, step, step + 1),
            block_forward(3 + step, trend_ref, 3 - step, 2 - step),
        ]
        yield from alternate(pair)
    for at, end in rows_in(0, ROWS, 16):
        joined = season_ref[at:end, lanes] + trend_ref[at:end, lanes]
        keep.joined[layer, at:end, lanes] = joined.astype(BF16)


def alternate(tasks):
    tasks = list(tasks)
    while tasks:
        for task in list(tasks):
            try:
                next(task)
            except StopIteration:
                tasks.remove(task)
        if tasks:
            yield


def run(*tasks):
    for _ in alternate(tasks):
        pass


def mixed_rows(item, first, last):
    start = item // GROUP * STEPS * GROUP + item % GROUP
    return pl.ds(start + GROUP * first, last - first, GROUP)


def lanes_of(item):
    return slice(item * WIDTH, (item + 1) * WIDTH)


def wide_of(item):
    return slice(item * HIDDEN, (item + 1) * HIDDEN)


def stacked(ref, lanes, items, *first):
    return jnp.concatenate([ref[first + (slice(None), lanes(i))] for i in items], axis=0)


def branch_forward(layer, weights, keep, items):
    before = dot(stacked(keep.joined, lanes_of, items, layer), weights.expand[layer])
    yield
    bias = weights.expand_bias[layer : layer + 1, :].astype(F32)
    for place, item in enumerate(items):
        for at, end in rows_in(0, ROWS, 32):
            piece = before[place * ROWS + at : place * ROWS + end]
            value, slope = gelu_and_slope(piece + bias)
            keep.hidden[layer, at:end, wide_of(item)] = value.astype(BF16)
            keep.hidden_slope[layer, at:end, wide_of(item)] = slope
            if end % 64 == 0:
                yield
    branch = dot(stacked(keep.hidden, wide_of, items, layer), weights.shrink[layer])
    yield
    bias = weights.shrink_bias[layer : layer + 1, :].astype(F32)
    for place, item in enumerate(items):
        lanes = lanes_of(item)
        for at, end, scale_at in PIECES:
            if layer == 0:
                value = keep.first_in[at:end, lanes]
            else:
                value = keep.second_in[at:end, lanes].astype(F32)
            residual = value + (branch[place * ROWS + at : place * ROWS + end] + bias)
            centred = residual - jnp.mean(residual, axis=-1, keepdims=True)
            scale = lax.rsqrt(jnp.mean(centred * centred, axis=-1, keepdims=True) + EPSILON)
            normed = centred * scale
            keep.normed[layer, at:end, lanes] = normed
            keep.scale[layer, at:end, lanes] = jnp.broadcast_to(scale, normed.shape)
            gain = weights.gain[layer, scale_at : scale_at + 1, :].astype(F32)
            value = normed * gain + weights.shift[layer, scale_at : scale_at + 1, :].astype(F32)
            if layer == 0:
                if end == ROWS:
                    value = jnp.where(iota(value.shape, 0) < STEPS - at, value, 0.0)
                if at == 144:
                    held = value
                elif at == 168:
                    value = jnp.concatenate([held, value], axis=0)
                    keep.second_in[144:end, lanes] = value.astype(BF16)
                else:
                    keep.second_in[at:end, lanes] = value.astype(BF16)
            else:
                last = min(end, STEPS)
                keep.output_mixed[mixed_rows(item, at, last), :] = value[: last - at]
        yield


def fold(value):
    return jnp.sum(value.reshape(value.shape[0] // 8, 8, value.shape[1]), axis=0)


def branch_backward(layer, weights, keep, items):
    for item in items:
        lanes = lanes_of(item)
        for at, end, scale_at in PIECES:
            upstream = keep.upstream[at:end, lanes]
            normed = keep.normed[layer, at:end, lanes]
            keep.vector[layer, 1 + scale_at] += fold(upstream * normed)
            keep.vector[layer, 5 + scale_at] += fold(upstream)
            graded = upstream * weights.gain[layer, scale_at : scale_at + 1, :].astype(F32)
            average = jnp.mean(graded, axis=-1, keepdims=True)
            along = jnp.mean(graded * normed, axis=-1, keepdims=True)
            residual = (graded - average - normed * along) * keep.scale[layer, at:end, lanes]
            keep.back_residual[at:end, lanes] = residual
            keep.vector[layer, 0] += fold(residual)
            if at == 144:
                held = residual
            elif at == 168:
                residual = jnp.concatenate([held, residual], axis=0)
                keep.back_low[144:end, lanes] = residual.astype(BF16)
            else:
                keep.back_low[at:end, lanes] = residual.astype(BF16)
        yield
    back = dot(stacked(keep.back_low, lanes_of, items), keep.shrink_back[layer])
    yield
    for place, item in enumerate(items):
        wide = wide_of(item)
        for at, end in rows_in(0, ROWS, 32):
            piece = back[place * ROWS + at : place * ROWS + end]
            value = piece * keep.hidden_slope[layer, at:end, wide]
            keep.hidden_bias[layer] += fold(value)
            keep.back_hidden[at:end, wide] = value.astype(BF16)
        yield
    back = dot(stacked(keep.back_hidden, wide_of, items), keep.expand_back[layer])
    yield
    for place, item in enumerate(items):
        keep.back_joined[:, lanes_of(item)] = back[place * ROWS : (place + 1) * ROWS]


def branch_sums(layer, keep, items):
    keep.grad_expand[layer] += dot_first(
        stacked(keep.joined, lanes_of, items, layer), stacked(keep.back_hidden, wide_of, items)
    )
    yield
    keep.grad_shrink[layer] += dot_first(
        stacked(keep.back_low, lanes_of, items), stacked(keep.hidden, wide_of, items, layer)
    )


def time_backward(layer, keep, lanes, items):
    season_ref, trend_ref = keep.season, keep.trend
    for at, end in rows_in(0, ROWS, 16):
        value = keep.back_joined[at:end, lanes]
        season_ref[at:end, lanes] = value
        trend_ref[at:end, lanes] = value

    def block_backward(block, value_ref, from_scale, to_scale):
        into, to = FROM[block], TO[block]
        rows, deep = ROWS_OF[to], DEEP[to]
        at, end = scale_rows(to_scale)
        low = padded(value_ref[at:end, lanes], to)
        back = dot(keep.leave_back[layer, TO_AT[block] : TO_AT[block] + rows, 0:deep], low)
        active = keep.active[layer, ACTIVE_AT[block] : ACTIVE_AT[block] + AUG[to], lanes]
        keep.grad_leave[layer, block, 0:deep, 0 : AUG[to]] += dot_last(low, active)
        yield
        slope_at = SLOPE_AT[block]
        back = [
            back[at:end] * keep.slope[layer, slope_at + at : slope_at + end, lanes]
            for at, end in rows_in(0, rows, 16)
        ]
        low = padded(jnp.concatenate(back, axis=0), to)
        at = FROM_AT[block]
        out = dot(keep.enter_back[layer, at : at + ROWS_OF[into], 0:deep], low)
        source = keep.source[layer, SOURCE_AT[block] : SOURCE_AT[block] + AUG[into], lanes]
        keep.grad_enter[layer, block, 0:deep, 0 : AUG[into]] += dot_last(low, source)
        yield
        start, _ = scale_rows(from_scale)
        for at, end in rows_in(0, ROWS_OF[into], 16):
            value_ref[start + at : start + end, lanes] += out[at:end]

    for step in range(3):
        pair = [
            block_backward(2 - step, season_ref, 2 - step, 3 - step),
            block_backward(5 - step, trend_ref, step + 1, step),
        ]
        yield from alternate(pair)
    for at, end in rows_in(0, ROWS, 16):
        value = trend_ref[at:end, lanes] - season_ref[at:end, lanes]
        keep.difference[at:end, lanes] = value.astype(BF16)
    averaged = dot(keep.means[1], keep.difference[:, lanes])
    yield
    for at, end in rows_in(0, ROWS, 16):
        value = keep.back_residual[at:end, lanes] + season_ref[at:end, lanes]
        value = value + averaged[at:end] * (1.0 / KERNEL)
        if layer == 1:
            keep.upstream[at:end, lanes] = value.astype(BF16).astype(F32)
        else:
            end = min(end, STEPS)
            for place, item in enumerate(items):
                target = mixed_rows(item, at, end)
                keep.back_mixed[target, :] = value[: end - at, lanes_of(place)]


def pack(keep, packed_ref):
    for layer in range(LAYERS):
        enter = [keep.grad_enter[layer, block] for block in range(6)]
        leave = [keep.grad_leave[layer, block] for block in range(6)]

        def moved(value, lanes):
            return pltpu.roll(value, lanes, 1)

        packed_ref[layer, 0:48, :] = enter[0][0:48]
        packed_ref[layer, 48:144, :] = leave[5][0:96]
        packed_ref[layer, 144:192, :] = leave[0][0:48] + moved(leave[4][0:48], 64)
        first = enter[5][0:48] + moved(enter[4][0:48], 64)
        narrow = jnp.concatenate(
            [
                moved(enter[2][0:16], 96),
                moved(leave[2][0:16], 96),
                jnp.zeros((16, WIDTH), F32),
            ],
            axis=0,
        )
        corner = jnp.concatenate(
            [
                jnp.zeros((16, WIDTH), F32),
                moved(enter[3][0:24], 112),
                jnp.zeros((8, WIDTH), F32),
            ],
            axis=0,
        )
        packed_ref[layer, 192:240, :] = first + narrow + corner
        packed_ref[layer, 240:264, :] = enter[5][48:72] + moved(enter[1][0:24], 64)
        packed_ref[layer, 264:288, :] = (
            enter[5][72:96] + moved(leave[1][0:24], 64) + moved(leave[3][0:24], 96)
        )
        vector = jnp.sum(keep.vector[layer], axis=1)
        hidden_bias = jnp.sum(keep.hidden_bias[layer], axis=0, keepdims=True)
        packed_ref[layer, VECTORS_AT:EXPAND_AT, :] = jnp.concatenate(
            [
                vector,
                hidden_bias[:, 0:WIDTH],
                hidden_bias[:, WIDTH:],
                jnp.zeros((5, WIDTH), F32),
            ],
            axis=0,
        )
        for side in range(2):
            lanes = slice(side * WIDTH, (side + 1) * WIDTH)
            at = EXPAND_AT + side * WIDTH
            packed_ref[layer, at : at + WIDTH, :] = keep.grad_expand[layer, :, lanes]
            at = SHRINK_AT + side * WIDTH
            packed_ref[layer, at : at + WIDTH, :] = keep.grad_shrink[layer, :, lanes]


CONSTANT = ("counts",)
SHARED = dict(expand=14, expand_bias=15, shrink=16, shrink_bias=17, gain=18, shift=19)
PREPARED = dict(
    means=((2, ROWS, ROWS), BF16),
    enter=((LAYERS, TO_ROWS, WIDTH), BF16),
    leave=((LAYERS, TO_ROWS, WIDTH), BF16),
    enter_back=((LAYERS, FROM_ROWS, WIDTH), BF16),
    leave_back=((LAYERS, TO_ROWS, WIDTH), BF16),
    expand_back=((LAYERS, HIDDEN, WIDTH), BF16),
    shrink_back=((LAYERS, WIDTH, HIDDEN), BF16),
)
MICROS = 2
CUT = 36
ITEMS = MICROS * GROUP
LANES = ITEMS * WIDTH
WORK = dict(
    split=((2 * ROWS, LANES), BF16),
    first_in=((ROWS, LANES), F32),
    second_in=((ROWS, LANES), BF16),
    season=((ROWS, LANES), F32),
    trend=((ROWS, LANES), F32),
    source=((LAYERS, SOURCE_ROWS, LANES), BF16),
    active=((LAYERS, ACTIVE_ROWS, LANES), BF16),
    slope=((LAYERS, SLOPE_ROWS, LANES), F32),
    joined=((LAYERS, ROWS, LANES), BF16),
    hidden=((LAYERS, ROWS, 2 * LANES), BF16),
    hidden_slope=((LAYERS, ROWS, 2 * LANES), F32),
    normed=((LAYERS, ROWS, LANES), F32),
    scale=((LAYERS, ROWS, LANES), F32),
    upstream=((ROWS, LANES), F32),
    back_residual=((ROWS, LANES), F32),
    back_low=((ROWS, LANES), BF16),
    back_hidden=((ROWS, 2 * LANES), BF16),
    back_joined=((ROWS, LANES), F32),
    difference=((ROWS, LANES), BF16),
    output_mixed=((STEPS * ITEMS, WIDTH), F32),
    back_mixed=((STEPS * ITEMS, WIDTH), F32),
    packed=((LAYERS, USED_ROWS, WIDTH), F32),
)
SUMS = dict(
    grad_enter=((LAYERS, 6, 96, WIDTH), F32),
    grad_leave=((LAYERS, 6, 96, WIDTH), F32),
    grad_expand=((LAYERS, WIDTH, HIDDEN), F32),
    grad_shrink=((LAYERS, WIDTH, HIDDEN), F32),
    vector=((LAYERS, 9, 8, WIDTH), F32),
    hidden_bias=((LAYERS, 8, HIDDEN), F32),
)
UNREAD = pl.BlockSpec(memory_space=pl.ANY)
STAGE = dict(stage=((LAYERS, 6, 2, 96, WIDTH), F32))


class Keep:
    def add(self, names, refs):
        for name, ref in zip(names, refs):
            setattr(self, name, ref)
        return refs[len(names) :]


def narrowed(source, micro, step, target):
    first = (micro * STEPS + step) * GROUP
    for at, end in rows_in(0, target.shape[0], 96):
        target[at:end, :] = source[first + at : first + end, :].astype(BF16)
        yield


def mixing_kernel(position_ref, input_ref, tangent_ref, *refs):
    keep, weights = Keep(), Keep()
    refs = keep.add(CONSTANT, refs)
    every, refs = refs[0:20], refs[20:]
    weights.add(SHARED, [every[at] for at in SHARED.values()])
    results, packed_ref, send_ref, refs = refs[0:3], refs[3], refs[4], refs[5:]
    refs = keep.add(SUMS, keep.add(WORK, keep.add(PREPARED, refs)))
    keep.add(STAGE, refs)
    prepare(every, keep)

    for name in SUMS:
        ref = getattr(keep, name)
        ref[...] = jnp.zeros(ref.shape, F32)
    tail = (iota((16, LANES), 0) == 0).astype(F32).astype(BF16)
    for layer in range(LAYERS):
        for block in range(6):
            for ref, at, length in (
                (keep.source, SOURCE_AT[block], FROM[block]),
                (keep.active, ACTIVE_AT[block], TO[block]),
            ):
                if length >= 48:
                    ref[layer, at + length : at + length + 16, :] = tail
    keep.first_in[176:ROWS, :] = jnp.zeros((16, LANES), F32)
    keep.upstream[176:ROWS, :] = jnp.zeros((16, LANES), F32)
    flat = input_ref.reshape(STEPS * ITEMS, WIDTH)
    for item in range(ITEMS):
        keep.first_in[0:STEPS, lanes_of(item)] = flat[mixed_rows(item, 0, STEPS), :]
    for at, end in rows_in(0, ROWS, 16):
        value = keep.first_in[at:end, :]
        high = value.astype(BF16)
        keep.split[at:end, :] = high
        keep.split[ROWS + at : ROWS + end, :] = (value - high.astype(F32)).astype(BF16)

    size = 4
    parts = [list(range(at, at + size)) for at in range(0, ITEMS, size)]

    def part_lanes(part):
        return slice(parts[part][0] * WIDTH, (parts[part][-1] + 1) * WIDTH)

    def mix(layer, part):
        return [time_forward(layer, keep, part_lanes(part))]

    def branch(layer, part):
        return [branch_forward(layer, weights, keep, parts[part])]

    def back_branch(layer, part):
        return [branch_backward(layer, weights, keep, parts[part])]

    def back_mix(layer, part):
        return [
            branch_sums(layer, keep, parts[part]),
            time_backward(layer, keep, part_lanes(part), parts[part]),
        ]

    stages = [(mix, 0), (branch, 0), (mix, 1), (branch, 1)]
    stages += [(back_branch, 1), (back_mix, 1), (back_branch, 0), (back_mix, 0)]
    flat = tangent_ref.reshape(STEPS * ITEMS, WIDTH)
    for item in range(ITEMS):
        keep.upstream[0:STEPS, lanes_of(item)] = flat[mixed_rows(item, 0, STEPS), :]
    places = tuple(enumerate(((0, 0), (1, 0), (1, CUT))))
    for turn in range(len(stages) + 1):
        tasks = []
        for part in range(len(parts)):
            if 0 <= turn - part % 2 < len(stages):
                stage, layer = stages[turn - part % 2]
                tasks += stage(layer, part)
        if turn == 5:
            tasks += [narrowed(keep.output_mixed, *place, results[i].at[0]) for i, place in places]
        run(*tasks)
    run(*(narrowed(keep.back_mixed, *place, results[i].at[1]) for i, place in places))

    pack(keep, keep.packed)
    core = jnp.bitwise_and(position_ref[0], 1)
    for at, end in rows_in(0, USED_ROWS, 16):
        for side, ref in enumerate((packed_ref, send_ref)):
            value = jnp.where(core == side, keep.packed[0, at:end], keep.packed[1, at:end])
            ref[at:end, :] = value.astype(BF16)


def whole(array):
    zeros = (0,) * len(array.shape)
    return pl.BlockSpec(array.shape, lambda *_: zeros, pipeline_mode=pl.Buffered(1))


def mixing(position, series_input, cotangent, weights, rows):
    shape = jax.ShapeDtypeStruct
    data = pl.BlockSpec(
        (MICROS, STEPS, GROUP, WIDTH),
        lambda _, at: (0, 0, at[0], 0),
        pipeline_mode=pl.Buffered(1),
    )
    average = moving_average()
    inputs = [jnp.asarray(np.stack([average, average.T])), *weights]
    lengths = (STEPS, CUT, STEPS - CUT)
    outs = [shape((2, steps * GROUP, WIDTH), BF16) for steps in lengths]
    outs += [shape((rows, WIDTH), BF16)] * 2
    scratch = [*PREPARED.values(), *WORK.values(), *SUMS.values(), *STAGE.values()]
    return pl.pallas_call(
        mixing_kernel,
        out_shape=tuple(outs),
        grid_spec=pltpu.PrefetchScalarGridSpec(
            num_scalar_prefetch=1,
            grid=(1,),
            in_specs=[data, data] + [whole(i) for i in inputs],
            out_specs=tuple(whole(o) for o in outs),
            scratch_shapes=[pltpu.VMEM(*spec) for spec in scratch],
        ),
        compiler_params=pltpu.CompilerParams(
            dimension_semantics=("arbitrary",), vmem_limit_bytes=61 * 2**20
        ),
        cost_estimate=pl.CostEstimate(
            flops=20_000_000_000, bytes_accessed=4_000_000, transcendentals=0
        ),
        name="mixing",
    )(position, series_input, cotangent, *inputs)


def unpack_kernel(position_ref, own_ref, other_ref, *outs):
    core = jnp.bitwise_and(position_ref[0], 1)
    own = own_ref[...].astype(F32).reshape(-1, WIDTH)
    other = other_ref[...].astype(F32).reshape(-1, WIDTH)

    def row_of(value, lane, at, lanes):
        column = value[:, lane : lane + 1]
        rows = value.shape[0]
        pick = iota((rows, lanes), 1) - at == iota((rows, lanes), 0)
        return jnp.sum(jnp.where(pick, column, 0.0), axis=0, keepdims=True)

    for layer in range(LAYERS):
        slab = jnp.where(core == layer, own, other)

        def back(rows, lanes):
            value = slab[rows]
            return pltpu.roll(value, WIDTH - lanes, 1) if lanes else value

        enter = [
            slab[0:48],
            back(slice(240, 264), 64),
            back(slice(192, 208), 96),
            back(slice(208, 232), 112),
            back(slice(192, 240), 64),
            slab[192:288],
        ]
        leave = [
            slab[144:192],
            back(slice(264, 288), 64),
            back(slice(208, 224), 96),
            back(slice(264, 288), 96),
            back(slice(144, 192), 64),
            slab[48:144],
        ]
        for block in range(6):
            rows, cols = TO[block], FROM[block]
            for arg, value, depth in (
                (ENTER_ARG[block], enter[block], cols),
                (LEAVE_ARG[block], leave[block], rows),
            ):
                value = value[0 : ROWS_OF[rows]]
                if arg in TURNED:
                    value = value.T[0:depth, 0:rows]
                else:
                    value = value[0:rows, 0:depth]
                if arg in MIDDLE:
                    outs[arg][:, layer, :] = value
                else:
                    outs[arg][layer] = value
        for blocks in ((0, 1, 2), (3, 4, 5)):
            target = outs[BIAS_ARG[blocks[0]]]
            lanes = target.shape[2]
            first = jnp.zeros((1, lanes), F32)
            second = jnp.zeros((1, lanes), F32)
            for block in blocks:
                rows = TO[block]
                first = first + row_of(enter[block][0:rows], FROM[block], BIAS_AT[block], lanes)
                second = second + row_of(leave[block][0:rows], TO[block], BIAS_AT[block], lanes)
            target[layer, 0:1, :] = first
            target[layer, 1:2, :] = second
        for side in range(2):
            lanes = slice(side * WIDTH, (side + 1) * WIDTH)
            at = EXPAND_AT + side * WIDTH
            outs[14][layer, :, lanes] = slab[at : at + WIDTH]
            at = SHRINK_AT + side * WIDTH
            outs[16][layer, lanes, :] = slab[at : at + WIDTH].T
        vector = slab[VECTORS_AT:EXPAND_AT]
        outs[17][layer : layer + 1, :] = vector[0:1]
        outs[18][layer] = vector[1:5]
        outs[19][layer] = vector[5:9]
        outs[15][layer : layer + 1, 0:WIDTH] = vector[9:10]
        outs[15][layer : layer + 1, WIDTH:] = vector[10:11]


def local_call(kernel, scalars, arrays, shapes, name, after=()):
    unread = [UNREAD] * len(after)
    return pl.pallas_call(
        kernel,
        out_shape=shapes,
        grid_spec=pltpu.PrefetchScalarGridSpec(
            num_scalar_prefetch=len(scalars),
            grid=(1,),
            in_specs=[whole(a) for a in arrays] + unread,
            out_specs=tuple(whole(s) for s in shapes),
        ),
        compiler_params=pltpu.CompilerParams(vmem_limit_bytes=16 * 2**20),
        name=name,
    )(*scalars, *arrays, *after)


def join_kernel(*refs):
    out_ref = refs[-1]
    rows = out_ref.shape[1]
    for part in range(out_ref.shape[0]):
        at = slice(part * rows, (part + 1) * rows)
        total = refs[0][at, :].astype(F32)
        for ref in refs[1:-1]:
            total = total + ref[at, :].astype(F32)
        out_ref[part] = total.astype(BF16)


def total_kernel(count, *refs):
    total = 0.0
    for ref in refs[0:count]:
        for part in range(ref.shape[0]):
            total = total + ref[part].astype(F32)
    total = total.astype(BF16)
    for part in range(refs[-1].shape[0]):
        refs[-1][part] = total


def added(parts, shape, after=()):
    kernel = functools.partial(total_kernel, len(parts))
    return local_call(kernel, (), parts, (shape,), "total", after)[0]


def hold_kernel(value_ref, after_ref, out_ref):
    pass


def hold(value, after):
    return pl.pallas_call(
        hold_kernel,
        out_shape=jax.ShapeDtypeStruct(value.shape, value.dtype),
        in_specs=[UNREAD, UNREAD],
        out_specs=UNREAD,
        input_output_aliases={0: 0},
        compiler_params=pltpu.CompilerParams(vmem_limit_bytes=16 * 2**20),
        name="hold",
    )(value, after)


def exchanged(value, axis):
    return lax.ppermute(value, axis, [(0, 1), (1, 0)])


def swapped(parts):
    return lax.all_to_all(parts, "dp", 0, 0, tiled=True)


def widen_kernel(position_ref, own_ref, other_ref, *refs):
    outs = refs[-3:-1]
    refs[-1][...] = jnp.zeros(refs[-1].shape, F32)
    core = jnp.bitwise_and(position_ref[0], 1)
    for kind in range(2):
        for turn, ref in enumerate((own_ref, other_ref)):
            at = pl.multiple_of(jnp.bitwise_xor(core, turn) * GROUP, GROUP)
            value = ref[kind].astype(F32).reshape(-1, GROUP, WIDTH)
            outs[kind][0, :, pl.ds(at, GROUP), :] = value


def widen(position, turn, micro, micros, start, parts, before=(), after=()):
    series = 2 * GROUP
    cut = parts[0].shape[1] // (CUT * GROUP)

    def chip(at):
        return jnp.bitwise_xor(jnp.right_shift(at[0], 1), turn)

    piece = pl.BlockSpec((2, CUT * GROUP, WIDTH), lambda t, at: (0, t, 0))
    out = pl.BlockSpec(
        (1, CUT, series, WIDTH), lambda t, at: (micro, start // CUT + t, chip(at), 0)
    )
    shape = jax.ShapeDtypeStruct((micros, STEPS, 2 * series, WIDTH), F32)
    token = jax.ShapeDtypeStruct((GROUP, WIDTH), F32)
    return pl.pallas_call(
        widen_kernel,
        out_shape=(shape, shape, token),
        grid_spec=pltpu.PrefetchScalarGridSpec(
            num_scalar_prefetch=1,
            grid=(cut,),
            in_specs=[piece] * 2 + [UNREAD] * (len(before) + len(after)),
            out_specs=(out, out, whole(token)),
        ),
        input_output_aliases={3: 0, 4: 1} if before else {},
        compiler_params=pltpu.CompilerParams(vmem_limit_bytes=16 * 2**20),
        name="widen",
    )(position, *parts, *before, *after)


def shards(series_input, cotangent, *weights):
    micros = series_input.shape[0]
    across, core = lax.axis_index("x"), lax.axis_index("core")
    position = (across * 2 + core).astype(jnp.int32).reshape(1)
    views = [jnp.transpose(w, ORDER[i]) if i in ORDER else w for i, w in enumerate(weights)]
    share = 8 * lax.axis_size("dp")
    rows = -(-USED_ROWS // share) * share
    first, early, late, packed, send = mixing(position, series_input, cotangent, views, rows)

    devices = lax.axis_size("dp")
    part = jax.ShapeDtypeStruct((1, rows // devices, WIDTH), BF16)
    parts = jax.ShapeDtypeStruct((devices, rows // devices, WIDTH), BF16)
    there = exchanged(first, "x")
    near = (first, exchanged(first, "core"))
    other = exchanged(send, "core")
    (sent,) = local_call(join_kernel, (), (packed, other), (parts,), "join")
    *outs, token = widen(position, 0, 0, micros, 0, near, (), (sent,))
    across = exchanged(early, "x")
    near = (early, exchanged(early, "core"))
    total = added((swapped(sent),), part, (token, across))
    summed = exchanged(total, "x")
    sent = added((total, summed), parts)

    late, held = hold(late, sent), hold(there, sent)
    there = exchanged(late, "x")
    far = (held, exchanged(held, "core"))
    *outs, token = widen(position, 1, 0, micros, 0, far, outs, (sent,))
    *outs, token = widen(position, 0, 1, micros, 0, near, outs, (sent,))
    held = hold(across, sent)
    far = (held, exchanged(held, "core"))
    *outs, token = widen(position, 1, 1, micros, 0, far, outs, (sent,))
    near = (late, exchanged(late, "core"))
    *outs, token = widen(position, 0, 1, micros, CUT, near, outs, (sent,))
    total = hold(swapped(sent), token)
    other = exchanged(total, "core")
    held = hold(there, other)
    far = (held, exchanged(held, "core"))
    *outs, token = widen(position, 1, 1, micros, CUT, far, outs)
    shapes = tuple(jax.ShapeDtypeStruct(v.shape, F32) for v in views)
    grads = local_call(unpack_kernel, (position,), (total, other), shapes, "unpack")
    turned = {i: tuple(order.index(d) for d in range(3)) for i, order in ORDER.items()}
    grads = [jnp.transpose(g, turned[i]) if i in turned else g for i, g in enumerate(grads)]
    return tuple(outs) + tuple(grads)


def solution(mesh):
    dp = mesh.shape["dp"]
    mesh = jax.sharding.Mesh(mesh.devices.reshape(dp, 2, 2), ("dp", "x", "core"))
    data = P(None, None, "dp", None)
    return jax.shard_map(
        shards,
        mesh=mesh,
        in_specs=(data, data) + (P(),) * 20,
        out_specs=(data, data) + (P(),) * 20,
        check_vma=False,
    )
```

time: 934 us -> 73.4 us (0.08); the launches traced: 920 us -> 73 us
  matrix products: 292 us -> 0 us
  waiting for transfers between devices: 258 us -> 12.1 us
  local copies, waits for them, and re-layouts: 200 us -> 2.05 us
  other arithmetic: 134 us -> 0 us
  Pallas kernels: 0 us -> 37.3 us
  between operations: 20.2 us -> 0.73 us
    dot_general x232 -> x0, matrix products: 292 us -> none  [the longest x60 83.8 us: contract_first(): lax.dot_general(left_side, right_side, (((0,), (0,)), ((), ())), preferre...]
    psum x4 -> x0, waiting for transfers between devices: 174 us -> none  [the longest x2 128 us: run_sections(): summed = lax.psum(running, 'dp')]
    reshape x84 -> x0, local copies, waits for them, and re-layouts: 93 us -> none  [the longest x35 54.1 us: layer_forward(): residual = pieces[scale_at].reshape(-1, features) + branch]
    all_gather x1 -> x0, waiting for transfers between devices: 43.7 us -> none  [run_sections(): lax.all_gather(own_piece.astype(jnp.bfloat16), 'pipe', axis=2, tiled=True)]
    reduce_sum x78 -> x0, other arithmetic: 41.8 us -> none  [the longest x22 17.2 us: normalize(): return centred * lax.rsqrt(spread + EPSILON) * gain_row + shift_row]
    pallas_call x0 -> x16, Pallas kernels: none -> 37.3 us  [the longest x1 22 us: mixing(): pl.pallas_call(mixing_kernel, out_shape=tuple(outs), grid_spec=pltpu.Pref...]
    unnamed x1091 -> x6, local copies, waits for them, and re-layouts: 33.7 us -> 2.05 us
    convert_element_type x29 -> x0, local copies, waits for them, and re-layouts: 30.5 us -> none  [the longest x20 19.1 us: layer_forward(): joined_low = (mixed_season[scale_at] + mixed_trend[scale_at]).reshape(-1,...]
  transfers between devices with their start and end apart: 9 -> 14, of which waited for: 9 -> 5; matrix products, arithmetic and copies ran while one was open for 8% -> 0% of each run, Pallas kernels for 0% -> 18%
where the time goes in v1:
time: 73.4 us; the launch traced here: 73 us
  Pallas kernels  37.3 us (51%)
  starting transfers between devices  20.8 us (28%)
  waiting for transfers between devices  12.1 us (16%)
  local copies, waits for them, and re-layouts  2.05 us (3%)
    pallas_call x1, Pallas kernels, mixing(): pl.pallas_call(mixing_kernel, out_shape=tuple(outs), grid_spec=pltpu.Pref...  22 us
    pallas_call x6, Pallas kernels, widen(): pl.pallas_call(widen_kernel, out_shape=(shape, shape, token), grid_spec=p...  12.6 us
    ppermute x12, waiting for transfers between devices, exchanged(): return lax.ppermute(value, axis, [(0, 1), (1, 0)])  12.1 us
    all_to_all x2, starting transfers between devices, swapped(): return lax.all_to_all(parts, 'dp', 0, 0, tiled=True)  11.7 us
    ppermute x12, starting transfers between devices, exchanged(): return lax.ppermute(value, axis, [(0, 1), (1, 0)])  9.11 us
    pallas_call x4, Pallas kernels, local_call(): pl.pallas_call(kernel, out_shape=shapes, grid_spec=pltpu.PrefetchScalarGr...  2.71 us
    unnamed x6, local copies, waits for them, and re-layouts  2.05 us
  transfers between devices with their start and end apart: 14, of which 5 were waited for; matrix products, arithmetic and copies ran while one was open for 0% of the time, Pallas kernels for 18%

profile of v1, /device:TPU:0, one launch (start us, length us, event | category | flops | bytes accessed | tf_op | source)
XLA Modules:
  0.0 73.0 jit_solution(17921945180382743693)
XLA Ops:
  0.7 22.0 %mixing.1 = (bf16[2,1440,128]{2,1,0:T(8,128)(2,1)}, bf16[2,288,128]{2,1,0:T(8,128)(2,1)}, bf16[2,1152,128]{2,1,0:T(8,128)(2,1)}, bf16[832,128]{1,0:T(8,128)(2,1)}, bf16[832,128]{1,0:T(8,128)(2,1)}) custom-call(s32[1]{0:T(128)} %bitcast.position_ref, f32[2,180,32,128]{3,2,1,0:T(8,128)} %input_ref.1, f32[2,180,32,128]{3,2,1,0:T(8,128)} %tangent_ref.1, ...), custom_call_target="tpu_custom_call" | custom-call | flops 20000000000 | bytes 4000000 | tf_op jit(solution)/shard_map/mixing/pallas_call | solution.py:629
  22.6 0.5 collective-permute-start.1
  23.2 2.6 %collective-permute-start.8 = (bf16[2,1440,128]{2,1,0:T(8,128)(2,1)}, bf16[2,1440,128]{2,1,0:T(8,128)(2,1)S(1)}, u32[]{:S(2)}, u32[]{:S(2)}) collective-permute-start(bf16[2,1440,128]{2,1,0:T(8,128)(2,1)} %get-tuple-element.64.own_ref), channel_id=1, source_target_pairs={{0,2},{2,0},{1,3},{3,1},{4,6},{6,4},{5,7},{7,5},{8,10},{10,8},{9,1... | collective-permute-start | bytes 2211848 | tf_op jit(solution)/shard_map/ppermute | solution.py:782
  25.7 0.2 collective-permute-start
  25.9 1.5 %collective-permute-done.refs_1_ = bf16[832,128]{1,0:T(8,128)(2,1)S(1)} collective-permute-done((bf16[832,128]{1,0:T(8,128)(2,1)}, bf16[832,128]{1,0:T(8,128)(2,1)S(1)}, u32[]{:S(2)}, u32[]{:S(2)}) %collective-permute-start) | collective-permute-done | bytes 213024 | tf_op jit(solution)/shard_map/ppermute | solution.py:782
  27.4 0.0 copy-start.1
  27.4 0.9 %copy-done.1 = bf16[832,128]{1,0:T(8,128)(2,1)S(1)} copy-done((bf16[832,128]{1,0:T(8,128)(2,1)S(1)}, bf16[832,128]{1,0:T(8,128)(2,1)}, u32[]{:S(2)}) %copy-start.1) | copy-done | bytes 213016
  28.3 0.0 copy-start.2
  28.3 0.7 %join.1.refs_0_ = bf16[8,104,128]{2,1,0:T(8,128)(2,1)} custom-call(bf16[832,128]{1,0:T(8,128)(2,1)S(1)} %copy-done.1, bf16[832,128]{1,0:T(8,128)(2,1)S(1)} %collective-permute-done.refs_1_), custom_call_target="tpu_custom_call" | custom-call | tf_op jit(solution)/shard_map/join/pallas_call | solution.py:725
  29.1 5.8 %all-to-all-start = ((bf16[8,104,128]{2,1,0:T(8,128)(2,1)}), bf16[8,104,128]{2,1,0:T(8,128)(2,1)S(1)}, u32[]{:S(2)}, u32[]{:S(2)}) async-start(bf16[8,104,128]{2,1,0:T(8,128)(2,1)} %join.1.refs_0_), calls=%async_computation | async-start | bytes 425984 | tf_op jit(solution)/shard_map/all_to_all | solution.py:786
  34.9 1.0 %collective-permute-start.2 = (bf16[2,288,128]{2,1,0:T(8,128)(2,1)}, bf16[2,288,128]{2,1,0:T(8,128)(2,1)S(1)}, u32[]{:S(2)}, u32[]{:S(2)}) collective-permute-start(bf16[2,288,128]{2,1,0:T(8,128)(2,1)} %get-tuple-element.66.own_ref), channel_id=1, source_target_pairs={{0,2},{2,0},{1,3},{3,1},{4,6},{6,4},{5,7},{7,5},{8,10},{10,8},{9,1... | collective-permute-start | bytes 442376 | tf_op jit(solution)/shard_map/ppermute | solution.py:782
  35.9 0.0 collective-permute-done.1.other_ref
  35.9 0.0 copy-start
  35.9 1.1 %copy-done = bf16[2,1440,128]{2,1,0:T(8,128)(2,1)S(1)} copy-done((bf16[2,1440,128]{2,1,0:T(8,128)(2,1)S(1)}, bf16[2,1440,128]{2,1,0:T(8,128)(2,1)}, u32[]{:S(2)}) %copy-start) | copy-done | bytes 737304
  37.0 2.7 %widen.6 = (f32[2,180,32,128]{3,2,1,0:T(8,128)}, f32[2,180,32,128]{3,2,1,0:T(8,128)}, f32[8,128]{1,0:T(8,128)S(1)}) custom-call(s32[1]{0:T(128)} %bitcast.position_ref, bf16[2,1440,128]{2,1,0:T(8,128)(2,1)S(1)} %copy-done, bf16[2,1440,128]{2,1,0:T(8,128)(2,1)S(1)} %collective-permute-done.1.other_ref, bf16[8,104,128]{2,1,0:T(8,128)(2,1)} %join.1.refs_0_), custom_call_target="tpu_custom_call" | custom-call | tf_op jit(solution)/shard_map/widen/pallas_call | solution.py:813
  39.7 6.5 %collective-permute-done.2.refs_2_.value_ref = bf16[2,288,128]{2,1,0:T(8,128)(2,1)S(1)} collective-permute-done((bf16[2,288,128]{2,1,0:T(8,128)(2,1)}, bf16[2,288,128]{2,1,0:T(8,128)(2,1)S(1)}, u32[]{:S(2)}, u32[]{:S(2)}) %collective-permute-start.2) | collective-permute-done | bytes 147488 | tf_op jit(solution)/shard_map/ppermute | solution.py:782
  46.2 0.0 all-to-all-done.refs_0_
  46.2 1.8 %collective-permute-start.3 = (bf16[1,104,128]{2,1,0:T(8,128)(2,1)S(1)}, bf16[1,104,128]{2,1,0:T(8,128)(2,1)S(1)}, u32[]{:S(2)}, u32[]{:S(2)}) collective-permute-start(bf16[1,104,128]{2,1,0:T(8,128)(2,1)S(1)} %total.2.refs_0_), channel_id=1, source_target_pairs={{0,2},{2,0},{1,3},{3,1},{4,6},{6,4},{5,7},{7,5},{8,10},{10,8},{9,1... | collective-permute-start | bytes 79880 | tf_op jit(solution)/shard_map/ppermute | solution.py:782
  48.0 2.1 %collective-permute-done.3.refs_1_ = bf16[1,104,128]{2,1,0:T(8,128)(2,1)S(1)} collective-permute-done((bf16[1,104,128]{2,1,0:T(8,128)(2,1)S(1)}, bf16[1,104,128]{2,1,0:T(8,128)(2,1)S(1)}, u32[]{:S(2)}, u32[]{:S(2)}) %collective-permute-start.3) | collective-permute-done | bytes 26656 | tf_op jit(solution)/shard_map/ppermute | solution.py:782
  50.1 0.7 total.3.after_ref.refs_2_
  50.8 0.0 collective-permute-done.8.value_ref
  50.8 0.0 collective-permute-start.9
  50.8 0.5 collective-permute-start.5
  51.3 1.8 %collective-permute-start.4 = (bf16[2,1152,128]{2,1,0:T(8,128)(2,1)}, bf16[2,1152,128]{2,1,0:T(8,128)(2,1)S(1)}, u32[]{:S(2)}, u32[]{:S(2)}) collective-permute-start(bf16[2,1152,128]{2,1,0:T(8,128)(2,1)} %hold.5.own_ref), channel_id=1, source_target_pairs={{0,2},{2,0},{1,3},{3,1},{4,6},{6,4},{5,7},{7,5},{8,10},{10,8},{9,1... | collective-permute-start | bytes 1769480 | tf_op jit(solution)/shard_map/ppermute | solution.py:782
  53.1 5.8 %all-to-all-start.1 = ((bf16[8,104,128]{2,1,0:T(8,128)(2,1)}), bf16[8,104,128]{2,1,0:T(8,128)(2,1)S(1)}, u32[]{:S(2)}, u32[]{:S(2)}) async-start(bf16[8,104,128]{2,1,0:T(8,128)(2,1)} %total.3.after_ref.refs_2_), calls=%async_computation.1 | async-start | bytes 425984 | tf_op jit(solution)/shard_map/all_to_all | solution.py:786
  58.9 0.0 copy-done.2
  58.9 0.1 collective-permute-start.7
  59.0 0.5 collective-permute-start.6
  59.5 0.0 collective-permute-done.9.other_ref
  59.5 2.7 %widen.7 = (f32[2,180,32,128]{3,2,1,0:T(8,128)}, f32[2,180,32,128]{3,2,1,0:T(8,128)}, f32[8,128]{1,0:T(8,128)}) custom-call(s32[1]{0:T(128)} %bitcast.position_ref, bf16[2,1440,128]{2,1,0:T(8,128)(2,1)S(1)} %hold.7.own_ref, bf16[2,1440,128]{2,1,0:T(8,128)(2,1)S(1)} %collective-permute-done.9.other_ref, ...), custom_call_target="tpu_custom_call", output_to_operand_aliasing={{0}: (3, {}), {1}: (4, {})} | custom-call | tf_op jit(solution)/shard_map/widen/pallas_call | solution.py:813
  62.2 0.0 collective-permute-done.7.other_ref
  62.2 0.9 %widen.8 = (f32[2,180,32,128]{3,2,1,0:T(8,128)}, f32[2,180,32,128]{3,2,1,0:T(8,128)}, f32[8,128]{1,0:T(8,128)}) custom-call(s32[1]{0:T(128)} %bitcast.position_ref, bf16[2,288,128]{2,1,0:T(8,128)(2,1)S(1)} %copy-done.2, bf16[2,288,128]{2,1,0:T(8,128)(2,1)S(1)} %collective-permute-done.7.other_ref, ...), custom_call_target="tpu_custom_call", output_to_operand_aliasing={{0}: (3, {}), {1}: (4, {})} | custom-call | tf_op jit(solution)/shard_map/widen/pallas_call | solution.py:813
  63.0 0.0 collective-permute-done.6.other_ref
  63.1 0.9 %widen.9 = (f32[2,180,32,128]{3,2,1,0:T(8,128)}, f32[2,180,32,128]{3,2,1,0:T(8,128)}, f32[8,128]{1,0:T(8,128)}) custom-call(s32[1]{0:T(128)} %bitcast.position_ref, bf16[2,288,128]{2,1,0:T(8,128)(2,1)S(1)} %hold.6.own_ref, bf16[2,288,128]{2,1,0:T(8,128)(2,1)S(1)} %collective-permute-done.6.other_ref, ...), custom_call_target="tpu_custom_call", output_to_operand_aliasing={{0}: (3, {}), {1}: (4, {})} | custom-call | tf_op jit(solution)/shard_map/widen/pallas_call | solution.py:813
  63.9 0.0 collective-permute-done.5.other_ref
  63.9 3.5 %widen.10 = (f32[2,180,32,128]{3,2,1,0:T(8,128)}, f32[2,180,32,128]{3,2,1,0:T(8,128)}, f32[8,128]{1,0:T(8,128)S(1)}) custom-call(s32[1]{0:T(128)} %bitcast.position_ref, bf16[2,1152,128]{2,1,0:T(8,128)(2,1)} %hold.5.own_ref, bf16[2,1152,128]{2,1,0:T(8,128)(2,1)S(1)} %collective-permute-done.5.other_ref, ...), custom_call_target="tpu_custom_call", output_to_operand_aliasing={{0}: (3, {}), {1}: (4, {})} | custom-call | tf_op jit(solution)/shard_map/widen/pallas_call | solution.py:813
  67.5 0.0 all-to-all-done.1.value_ref
  67.5 0.1 collective-permute-start.10
  67.6 0.0 collective-permute-done.4.value_ref
  67.6 1.4 %collective-permute-done.10.after_ref.other_ref = bf16[8,104,128]{2,1,0:T(8,128)(2,1)S(1)} collective-permute-done((bf16[8,104,128]{2,1,0:T(8,128)(2,1)S(1)}, bf16[8,104,128]{2,1,0:T(8,128)(2,1)S(1)}, u32[]{:S(2)}, u32[]{:S(2)}) %collective-permute-start.10) | collective-permute-done | bytes 213024 | tf_op jit(solution)/shard_map/ppermute | solution.py:782
  68.9 0.1 collective-permute-start.11
  69.1 1.2 %unpack.1 = (f32[2,48,96]{2,1,0:T(8,128)}, f32[2,24,48]{2,1,0:T(8,128)}, f32[12,2,24]{2,1,0:T(2,128)}, f32[2,48,48]{2,1,0:T(8,128)}, f32[2,24,24]{2,1,0:T(8,128)...) custom-call(s32[1]{0:T(128)} %bitcast.position_ref, ...), custom_call_target="tpu_custom_call" | custom-call | tf_op jit(solution)/shard_map/unpack/pallas_call | solution.py:725
  70.3 0.6 collective-permute-done.11.other_ref
  70.9 2.0 %widen.11 = (f32[2,180,32,128]{3,2,1,0:T(8,128)}, f32[2,180,32,128]{3,2,1,0:T(8,128)}, f32[8,128]{1,0:T(8,128)}) custom-call(s32[1]{0:T(128)} %bitcast.position_ref, bf16[2,1152,128]{2,1,0:T(8,128)(2,1)S(1)} %hold.9.own_ref, bf16[2,1152,128]{2,1,0:T(8,128)(2,1)S(1)} %collective-permute-done.11.other_ref, ...), custom_call_target="tpu_custom_call", output_to_operand_aliasing={{0}: (3, {}), {1}: (4, {})} | custom-call | tf_op jit(solution)/shard_map/widen/pallas_call | solution.py:813
  (6 shorter events, 0.0 us)
Async XLA Ops:
  22.6 13.2 %collective-permute-start.1 = (bf16[2,1440,128]{2,1,0:T(8,128)(2,1)}, bf16[2,1440,128]{2,1,0:T(8,128)(2,1)S(1)}, u32[]{:S(2)}, u32[]{:S(2)}) collective-permute-start(bf16[2,1440,128]{2,1,0:T(8,128)(2,1)} %get-tuple-element.64.own_ref), channel_id=1, source_target_pairs={{0,1},{1,0},{2,3},{3,2},{4,5},{5,4},{6,7},{7,6},{8,9},{9,8},{10,11... | collective-permute-start | bytes 2211848 | tf_op jit(solution)/shard_map/ppermute | solution.py:782
  23.2 27.7 %collective-permute-start.8 = (bf16[2,1440,128]{2,1,0:T(8,128)(2,1)}, bf16[2,1440,128]{2,1,0:T(8,128)(2,1)S(1)}, u32[]{:S(2)}, u32[]{:S(2)}) collective-permute-start(bf16[2,1440,128]{2,1,0:T(8,128)(2,1)} %get-tuple-element.64.own_ref), channel_id=1, source_target_pairs={{0,2},{2,0},{1,3},{3,1},{4,6},{6,4},{5,7},{7,5},{8,10},{10,8},{9,1... | collective-permute-start | bytes 2211848 | tf_op jit(solution)/shard_map/ppermute | solution.py:782
  25.7 1.7 %collective-permute-start = (bf16[832,128]{1,0:T(8,128)(2,1)}, bf16[832,128]{1,0:T(8,128)(2,1)S(1)}, u32[]{:S(2)}, u32[]{:S(2)}) collective-permute-start(bf16[832,128]{1,0:T(8,128)(2,1)} %get-tuple-element.63), channel_id=1, source_target_pairs={{0,1},{1,0},{2,3},{3,2},{4,5},{5,4},{6,7},{7,6},{8,9},{9,8},{10,11... | collective-permute-start | bytes 638984 | tf_op jit(solution)/shard_map/ppermute | solution.py:782
  27.4 0.9 %copy-start.1 = (bf16[832,128]{1,0:T(8,128)(2,1)S(1)}, bf16[832,128]{1,0:T(8,128)(2,1)}, u32[]{:S(2)}) copy-start(bf16[832,128]{1,0:T(8,128)(2,1)} %get-tuple-element.62.refs_0_) | copy-start | bytes 638980
  28.3 30.6 %copy-start.2 = (bf16[2,288,128]{2,1,0:T(8,128)(2,1)S(1)}, bf16[2,288,128]{2,1,0:T(8,128)(2,1)}, u32[]{:S(2)}) copy-start(bf16[2,288,128]{2,1,0:T(8,128)(2,1)} %get-tuple-element.66.own_ref) | copy-start | bytes 442372
  29.1 17.1 %all-to-all-start = ((bf16[8,104,128]{2,1,0:T(8,128)(2,1)}), bf16[8,104,128]{2,1,0:T(8,128)(2,1)S(1)}, u32[]{:S(2)}, u32[]{:S(2)}) async-start(bf16[8,104,128]{2,1,0:T(8,128)(2,1)} %join.1.refs_0_), calls=%async_computation | async-start | bytes 425984 | tf_op jit(solution)/shard_map/all_to_all | solution.py:786
  34.9 11.3 %collective-permute-start.2 = (bf16[2,288,128]{2,1,0:T(8,128)(2,1)}, bf16[2,288,128]{2,1,0:T(8,128)(2,1)S(1)}, u32[]{:S(2)}, u32[]{:S(2)}) collective-permute-start(bf16[2,288,128]{2,1,0:T(8,128)(2,1)} %get-tuple-element.66.own_ref), channel_id=1, source_target_pairs={{0,2},{2,0},{1,3},{3,1},{4,6},{6,4},{5,7},{7,5},{8,10},{10,8},{9,1... | collective-permute-start | bytes 442376 | tf_op jit(solution)/shard_map/ppermute | solution.py:782
  35.9 1.1 %copy-start = (bf16[2,1440,128]{2,1,0:T(8,128)(2,1)S(1)}, bf16[2,1440,128]{2,1,0:T(8,128)(2,1)}, u32[]{:S(2)}) copy-start(bf16[2,1440,128]{2,1,0:T(8,128)(2,1)} %get-tuple-element.64.own_ref) | copy-start | bytes 2211844
  46.2 3.9 %collective-permute-start.3 = (bf16[1,104,128]{2,1,0:T(8,128)(2,1)S(1)}, bf16[1,104,128]{2,1,0:T(8,128)(2,1)S(1)}, u32[]{:S(2)}, u32[]{:S(2)}) collective-permute-start(bf16[1,104,128]{2,1,0:T(8,128)(2,1)S(1)} %total.2.refs_0_), channel_id=1, source_target_pairs={{0,2},{2,0},{1,3},{3,1},{4,6},{6,4},{5,7},{7,5},{8,10},{10,8},{9,1... | collective-permute-start | bytes 79880 | tf_op jit(solution)/shard_map/ppermute | solution.py:782
  50.8 8.7 %collective-permute-start.9 = (bf16[2,1440,128]{2,1,0:T(8,128)(2,1)S(1)}, bf16[2,1440,128]{2,1,0:T(8,128)(2,1)S(1)}, u32[]{:S(2)}, u32[]{:S(2)}) collective-permute-start(bf16[2,1440,128]{2,1,0:T(8,128)(2,1)S(1)} %hold.7.own_ref), channel_id=1, source_target_pairs={{0,1},{1,0},{2,3},{3,2},{4,5},{5,4},{6,7},{7,6},{8,9},{9,8},{10,11... | collective-permute-start | bytes 2211848 | tf_op jit(solution)/shard_map/ppermute | solution.py:782
  50.8 13.1 %collective-permute-start.5 = (bf16[2,1152,128]{2,1,0:T(8,128)(2,1)}, bf16[2,1152,128]{2,1,0:T(8,128)(2,1)S(1)}, u32[]{:S(2)}, u32[]{:S(2)}) collective-permute-start(bf16[2,1152,128]{2,1,0:T(8,128)(2,1)} %hold.5.own_ref), channel_id=1, source_target_pairs={{0,1},{1,0},{2,3},{3,2},{4,5},{5,4},{6,7},{7,6},{8,9},{9,8},{10,11... | collective-permute-start | bytes 1769480 | tf_op jit(solution)/shard_map/ppermute | solution.py:782
  51.3 16.2 %collective-permute-start.4 = (bf16[2,1152,128]{2,1,0:T(8,128)(2,1)}, bf16[2,1152,128]{2,1,0:T(8,128)(2,1)S(1)}, u32[]{:S(2)}, u32[]{:S(2)}) collective-permute-start(bf16[2,1152,128]{2,1,0:T(8,128)(2,1)} %hold.5.own_ref), channel_id=1, source_target_pairs={{0,2},{2,0},{1,3},{3,1},{4,6},{6,4},{5,7},{7,5},{8,10},{10,8},{9,1... | collective-permute-start | bytes 1769480 | tf_op jit(solution)/shard_map/ppermute | solution.py:782
  53.1 14.4 %all-to-all-start.1 = ((bf16[8,104,128]{2,1,0:T(8,128)(2,1)}), bf16[8,104,128]{2,1,0:T(8,128)(2,1)S(1)}, u32[]{:S(2)}, u32[]{:S(2)}) async-start(bf16[8,104,128]{2,1,0:T(8,128)(2,1)} %total.3.after_ref.refs_2_), calls=%async_computation.1 | async-start | bytes 425984 | tf_op jit(solution)/shard_map/all_to_all | solution.py:786
  58.9 3.3 %collective-permute-start.7 = (bf16[2,288,128]{2,1,0:T(8,128)(2,1)S(1)}, bf16[2,288,128]{2,1,0:T(8,128)(2,1)S(1)}, u32[]{:S(2)}, u32[]{:S(2)}) collective-permute-start(bf16[2,288,128]{2,1,0:T(8,128)(2,1)S(1)} %copy-done.2), channel_id=1, source_target_pairs={{0,1},{1,0},{2,3},{3,2},{4,5},{5,4},{6,7},{7,6},{8,9},{9,8},{10,11... | collective-permute-start | bytes 442376 | tf_op jit(solution)/shard_map/ppermute | solution.py:782
  59.0 4.0 %collective-permute-start.6 = (bf16[2,288,128]{2,1,0:T(8,128)(2,1)S(1)}, bf16[2,288,128]{2,1,0:T(8,128)(2,1)S(1)}, u32[]{:S(2)}, u32[]{:S(2)}) collective-permute-start(bf16[2,288,128]{2,1,0:T(8,128)(2,1)S(1)} %hold.6.own_ref), channel_id=1, source_target_pairs={{0,1},{1,0},{2,3},{3,2},{4,5},{5,4},{6,7},{7,6},{8,9},{9,8},{10,11... | collective-permute-start | bytes 442376 | tf_op jit(solution)/shard_map/ppermute | solution.py:782
  67.5 1.5 %collective-permute-start.10 = (bf16[8,104,128]{2,1,0:T(8,128)(2,1)S(1)}, bf16[8,104,128]{2,1,0:T(8,128)(2,1)S(1)}, u32[]{:S(2)}, u32[]{:S(2)}) collective-permute-start(bf16[8,104,128]{2,1,0:T(8,128)(2,1)S(1)} %hold.8.own_ref), channel_id=1, source_target_pairs={{0,1},{1,0},{2,3},{3,2},{4,5},{5,4},{6,7},{7,6},{8,9},{9,8},{10,11... | collective-permute-start | bytes 638984 | tf_op jit(solution)/shard_map/ppermute | solution.py:782
  68.9 2.0 %collective-permute-start.11 = (bf16[2,1152,128]{2,1,0:T(8,128)(2,1)S(1)}, bf16[2,1152,128]{2,1,0:T(8,128)(2,1)S(1)}, u32[]{:S(2)}, u32[]{:S(2)}) collective-permute-start(bf16[2,1152,128]{2,1,0:T(8,128)(2,1)S(1)} %hold.9.own_ref), channel_id=1, source_target_pairs={{0,1},{1,0},{2,3},{3,2},{4,5},{5,4},{6,7},{7,6},{8,9},{9,8},{10,11... | collective-permute-start | bytes 1769480 | tf_op jit(solution)/shard_map/ppermute | solution.py:782

commit v2 on v1

--- a/solution.py
+++ b/solution.py
@@ -476,7 +476,6 @@
     shrink_back=((LAYERS, WIDTH, HIDDEN), BF16),
 )
 MICROS = 2
-CUT = 36
 ITEMS = MICROS * GROUP
 LANES = ITEMS * WIDTH
 WORK = dict(
@@ -522,9 +521,9 @@
         return refs[len(names) :]
 
 
-def narrowed(source, micro, step, target):
-    first = (micro * STEPS + step) * GROUP
-    for at, end in rows_in(0, target.shape[0], 96):
+def narrowed(source, micro, target):
+    first = micro * STEPS * GROUP
+    for at, end in rows_in(0, STEPS * GROUP, 96):
         target[at:end, :] = source[first + at : first + end, :].astype(BF16)
         yield
 
@@ -534,7 +533,7 @@
     refs = keep.add(CONSTANT, refs)
     every, refs = refs[0:20], refs[20:]
     weights.add(SHARED, [every[at] for at in SHARED.values()])
-    results, packed_ref, send_ref, refs = refs[0:3], refs[3], refs[4], refs[5:]
+    results, packed_ref, send_ref, refs = refs[0:MICROS], *refs[MICROS : MICROS + 2], refs[4:]
     refs = keep.add(SUMS, keep.add(WORK, keep.add(PREPARED, refs)))
     keep.add(STAGE, refs)
     prepare(every, keep)
@@ -588,7 +587,6 @@
     flat = tangent_ref.reshape(STEPS * ITEMS, WIDTH)
     for item in range(ITEMS):
         keep.upstream[0:STEPS, lanes_of(item)] = flat[mixed_rows(item, 0, STEPS), :]
-    places = tuple(enumerate(((0, 0), (1, 0), (1, CUT))))
     for turn in range(len(stages) + 1):
         tasks = []
         for part in range(len(parts)):
@@ -596,9 +594,9 @@
                 stage, layer = stages[turn - part % 2]
                 tasks += stage(layer, part)
         if turn == 5:
-            tasks += [narrowed(keep.output_mixed, *place, results[i].at[0]) for i, place in places]
+            tasks += [narrowed(keep.output_mixed, m, results[m].at[0]) for m in range(MICROS)]
         run(*tasks)
-    run(*(narrowed(keep.back_mixed, *place, results[i].at[1]) for i, place in places))
+    run(*(narrowed(keep.back_mixed, m, results[m].at[1]) for m in range(MICROS)))
 
     pack(keep, keep.packed)
     core = jnp.bitwise_and(position_ref[0], 1)
@@ -622,9 +620,7 @@
     )
     average = moving_average()
     inputs = [jnp.asarray(np.stack([average, average.T])), *weights]
-    lengths = (STEPS, CUT, STEPS - CUT)
-    outs = [shape((2, steps * GROUP, WIDTH), BF16) for steps in lengths]
-    outs += [shape((rows, WIDTH), BF16)] * 2
+    outs = [shape((2, STEPS * GROUP, WIDTH), BF16)] * MICROS + [shape((rows, WIDTH), BF16)] * 2
     scratch = [*PREPARED.values(), *WORK.values(), *SUMS.values(), *STAGE.values()]
     return pl.pallas_call(
         mixing_kernel,
@@ -797,17 +793,15 @@
             outs[kind][0, :, pl.ds(at, GROUP), :] = value
 
 
-def widen(position, turn, micro, micros, start, parts, before=(), after=()):
+def widen(position, turn, micro, micros, parts, before=(), after=()):
     series = 2 * GROUP
-    cut = parts[0].shape[1] // (CUT * GROUP)
+    cut = 4
 
     def chip(at):
         return jnp.bitwise_xor(jnp.right_shift(at[0], 1), turn)
 
-    piece = pl.BlockSpec((2, CUT * GROUP, WIDTH), lambda t, at: (0, t, 0))
-    out = pl.BlockSpec(
-        (1, CUT, series, WIDTH), lambda t, at: (micro, start // CUT + t, chip(at), 0)
-    )
+    piece = pl.BlockSpec((2, STEPS * GROUP // cut, WIDTH), lambda t, at: (0, t, 0))
+    out = pl.BlockSpec((1, STEPS // cut, series, WIDTH), lambda t, at: (micro, t, chip(at), 0))
     shape = jax.ShapeDtypeStruct((micros, STEPS, 2 * series, WIDTH), F32)
     token = jax.ShapeDtypeStruct((GROUP, WIDTH), F32)
     return pl.pallas_call(
@@ -832,7 +826,7 @@
     views = [jnp.transpose(w, ORDER[i]) if i in ORDER else w for i, w in enumerate(weights)]
     share = 8 * lax.axis_size("dp")
     rows = -(-USED_ROWS // share) * share
-    first, early, late, packed, send = mixing(position, series_input, cotangent, views, rows)
+    first, second, packed, send = mixing(position, series_input, cotangent, views, rows)
 
     devices = lax.axis_size("dp")
     part = jax.ShapeDtypeStruct((1, rows // devices, WIDTH), BF16)
@@ -841,28 +835,22 @@
     near = (first, exchanged(first, "core"))
     other = exchanged(send, "core")
     (sent,) = local_call(join_kernel, (), (packed, other), (parts,), "join")
-    *outs, token = widen(position, 0, 0, micros, 0, near, (), (sent,))
-    across = exchanged(early, "x")
-    near = (early, exchanged(early, "core"))
-    total = added((swapped(sent),), part, (token, across))
-    summed = exchanged(total, "x")
-    sent = added((total, summed), parts)
-
-    late, held = hold(late, sent), hold(there, sent)
-    there = exchanged(late, "x")
+    *outs, token = widen(position, 0, 0, micros, near, (), (sent,))
+    total = added((swapped(sent),), part, (token,))
+    across = exchanged(total, "x")
+    sent = added((total, across), parts)
+
+    second, held = hold(second, sent), hold(there, sent)
     far = (held, exchanged(held, "core"))
-    *outs, token = widen(position, 1, 0, micros, 0, far, outs, (sent,))
-    *outs, token = widen(position, 0, 1, micros, 0, near, outs, (sent,))
-    held = hold(across, sent)
-    far = (held, exchanged(held, "core"))
-    *outs, token = widen(position, 1, 1, micros, 0, far, outs, (sent,))
-    near = (late, exchanged(late, "core"))
-    *outs, token = widen(position, 0, 1, micros, CUT, near, outs, (sent,))
+    *outs, token = widen(position, 1, 0, micros, far, outs, (sent,))
+    there = exchanged(second, "x")
+    near = (second, exchanged(second, "core"))
+    *outs, token = widen(position, 0, 1, micros, near, outs, (sent,))
     total = hold(swapped(sent), token)
     other = exchanged(total, "core")
     held = hold(there, other)
     far = (held, exchanged(held, "core"))
-    *outs, token = widen(position, 1, 1, micros, CUT, far, outs)
+    *outs, token = widen(position, 1, 1, micros, far, outs)
     shapes = tuple(jax.ShapeDtypeStruct(v.shape, F32) for v in views)
     grads = local_call(unpack_kernel, (position,), (total, other), shapes, "unpack")
     turned = {i: tuple(order.index(d) for d in range(3)) for i, order in ORDER.items()}

time: 73.4 us -> 72.1 us (0.982)
  waiting for transfers between devices: 12.1 us -> 19 us
  starting transfers between devices: 20.8 us -> 15 us
  Pallas kernels: 37.3 us -> 35 us
    all_to_all x2, waiting for transfers between devices: 0.01 us -> 7.62 us  [swapped(): return lax.all_to_all(parts, 'dp', 0, 0, tiled=True)]
    ppermute x12 -> x9, starting transfers between devices: 9.11 us -> 5.72 us  [exchanged(): return lax.ppermute(value, axis, [(0, 1), (1, 0)])]
    all_to_all x2, starting transfers between devices: 11.7 us -> 9.23 us  [swapped(): return lax.all_to_all(parts, 'dp', 0, 0, tiled=True)]
    pallas_call x6 -> x4, Pallas kernels: 12.6 us -> 10.3 us  [widen(): pl.pallas_call(widen_kernel, out_shape=(shape, shape, token), grid_spec=p...]
    ppermute x12 -> x9, waiting for transfers between devices: 12.1 us -> 11.3 us  [exchanged(): return lax.ppermute(value, axis, [(0, 1), (1, 0)])]
    unnamed x6 -> x4, local copies, waits for them, and re-layouts: 2.05 us -> 2.04 us
  transfers between devices with their start and end apart: 14 -> 11, of which waited for: 5 -> 6; matrix products, arithmetic and copies ran while one was open for 0% -> 0% of each run, Pallas kernels for 18% -> 15%
where the time goes in v2:
time: 72.1 us; the launch traced here: 71.6 us
  Pallas kernels  35 us (49%)
  waiting for transfers between devices  19 us (26%)
  starting transfers between devices  15 us (21%)
  local copies, waits for them, and re-layouts  2.04 us (3%)
  between operations  0.73 us (1%)
    pallas_call x1, Pallas kernels, mixing(): pl.pallas_call(mixing_kernel, out_shape=tuple(outs), grid_spec=pltpu.Pref...  21.9 us
    ppermute x9, waiting for transfers between devices, exchanged(): return lax.ppermute(value, axis, [(0, 1), (1, 0)])  11.3 us
    pallas_call x4, Pallas kernels, widen(): pl.pallas_call(widen_kernel, out_shape=(shape, shape, token), grid_spec=p...  10.3 us
    all_to_all x2, starting transfers between devices, swapped(): return lax.all_to_all(parts, 'dp', 0, 0, tiled=True)  9.23 us
    all_to_all x2, waiting for transfers between devices, swapped(): return lax.all_to_all(parts, 'dp', 0, 0, tiled=True)  7.62 us
    ppermute x9, starting transfers between devices, exchanged(): return lax.ppermute(value, axis, [(0, 1), (1, 0)])  5.72 us
    pallas_call x4, Pallas kernels, local_call(): pl.pallas_call(kernel, out_shape=shapes, grid_spec=pltpu.PrefetchScalarGr...  2.72 us
    unnamed x4, local copies, waits for them, and re-layouts  2.04 us
  transfers between devices with their start and end apart: 11, of which 6 were waited for; matrix products, arithmetic and copies ran while one was open for 0% of the time, Pallas kernels for 15%

profile of v2, /device:TPU:0, one launch (start us, length us, event | category | flops | bytes accessed | tf_op | source)
XLA Modules:
  0.0 71.6 jit_solution(4685646772256301000)
XLA Ops:
  0.7 21.9 %mixing.1 = (bf16[2,1440,128]{2,1,0:T(8,128)(2,1)}, bf16[2,1440,128]{2,1,0:T(8,128)(2,1)}, bf16[832,128]{1,0:T(8,128)(2,1)}, bf16[832,128]{1,0:T(8,128)(2,1)}) custom-call(s32[1]{0:T(128)} %bitcast.position_ref, f32[2,180,32,128]{3,2,1,0:T(8,128)} %input_ref.1, f32[2,180,32,128]{3,2,1,0:T(8,128)} %tangent_ref.1, f32[2,192,192]{2,1,0:T(8,128)} %constant.10.clone.refs_0_, ...), custom_call_target="tpu_custom_call" | custom-call | flops 20000000000 | bytes 4000000 | tf_op jit(solution)/shard_map/mixing/pallas_call | solution.py:625
  22.6 0.5 collective-permute-start.1
  23.1 2.6 %collective-permute-start.5 = (bf16[2,1440,128]{2,1,0:T(8,128)(2,1)}, bf16[2,1440,128]{2,1,0:T(8,128)(2,1)S(1)}, u32[]{:S(2)}, u32[]{:S(2)}) collective-permute-start(bf16[2,1440,128]{2,1,0:T(8,128)(2,1)} %get-tuple-element.59.own_ref), channel_id=1, source_target_pairs={{0,2},{2,0},{1,3},{3,1},{4,6},{6,4},{5,7},{7,5},{8,10},{10,8},{9,1... | collective-permute-start | bytes 2211848 | tf_op jit(solution)/shard_map/ppermute | solution.py:778
  25.7 0.2 collective-permute-start
  25.8 1.5 %collective-permute-done.refs_1_ = bf16[832,128]{1,0:T(8,128)(2,1)S(1)} collective-permute-done((bf16[832,128]{1,0:T(8,128)(2,1)}, bf16[832,128]{1,0:T(8,128)(2,1)S(1)}, u32[]{:S(2)}, u32[]{:S(2)}) %collective-permute-start) | collective-permute-done | bytes 213024 | tf_op jit(solution)/shard_map/ppermute | solution.py:778
  27.4 0.0 copy-start.1
  27.4 0.9 %copy-done.1 = bf16[832,128]{1,0:T(8,128)(2,1)S(1)} copy-done((bf16[832,128]{1,0:T(8,128)(2,1)S(1)}, bf16[832,128]{1,0:T(8,128)(2,1)}, u32[]{:S(2)}) %copy-start.1) | copy-done | bytes 213016
  28.3 0.7 %join.1.refs_0_ = bf16[8,104,128]{2,1,0:T(8,128)(2,1)} custom-call(bf16[832,128]{1,0:T(8,128)(2,1)S(1)} %copy-done.1, bf16[832,128]{1,0:T(8,128)(2,1)S(1)} %collective-permute-done.refs_1_), custom_call_target="tpu_custom_call" | custom-call | tf_op jit(solution)/shard_map/join/pallas_call | solution.py:721
  29.0 5.8 %all-to-all-start = ((bf16[8,104,128]{2,1,0:T(8,128)(2,1)}), bf16[8,104,128]{2,1,0:T(8,128)(2,1)S(1)}, u32[]{:S(2)}, u32[]{:S(2)}) async-start(bf16[8,104,128]{2,1,0:T(8,128)(2,1)} %join.1.refs_0_), calls=%async_computation | async-start | bytes 425984 | tf_op jit(solution)/shard_map/all_to_all | solution.py:782
  34.9 0.0 collective-permute-done.1.other_ref
  34.9 0.0 copy-start
  34.9 1.1 %copy-done = bf16[2,1440,128]{2,1,0:T(8,128)(2,1)S(1)} copy-done((bf16[2,1440,128]{2,1,0:T(8,128)(2,1)S(1)}, bf16[2,1440,128]{2,1,0:T(8,128)(2,1)}, u32[]{:S(2)}) %copy-start) | copy-done | bytes 737304
  36.0 2.2 %widen.4 = (f32[2,180,32,128]{3,2,1,0:T(8,128)}, f32[2,180,32,128]{3,2,1,0:T(8,128)}, f32[8,128]{1,0:T(8,128)S(1)}) custom-call(s32[1]{0:T(128)} %bitcast.position_ref, bf16[2,1440,128]{2,1,0:T(8,128)(2,1)S(1)} %copy-done, bf16[2,1440,128]{2,1,0:T(8,128)(2,1)S(1)} %collective-permute-done.1.other_ref, bf16[8,104,128]{2,1,0:T(8,128)(2,1)} %join.1.refs_0_), custom_call_target="tpu_custom_call" | custom-call | tf_op jit(solution)/shard_map/widen/pallas_call | solution.py:807
  38.2 5.2 %all-to-all-done.refs_0_ = bf16[8,104,128]{2,1,0:T(8,128)(2,1)S(1)} async-done(((bf16[8,104,128]{2,1,0:T(8,128)(2,1)}), bf16[8,104,128]{2,1,0:T(8,128)(2,1)S(1)}, u32[]{:S(2)}, u32[]{:S(2)}) %all-to-all-start) | async-done | bytes 213024 | tf_op jit(solution)/shard_map/all_to_all | solution.py:782
  43.4 1.0 %collective-permute-start.2 = (bf16[1,104,128]{2,1,0:T(8,128)(2,1)S(1)}, bf16[1,104,128]{2,1,0:T(8,128)(2,1)S(1)}, u32[]{:S(2)}, u32[]{:S(2)}) collective-permute-start(bf16[1,104,128]{2,1,0:T(8,128)(2,1)S(1)} %total.2.refs_0_), channel_id=1, source_target_pairs={{0,2},{2,0},{1,3},{3,1},{4,6},{6,4},{5,7},{7,5},{8,10},{10,8},{9,1... | collective-permute-start | bytes 79880 | tf_op jit(solution)/shard_map/ppermute | solution.py:778
  44.4 2.9 %collective-permute-done.2.refs_1_ = bf16[1,104,128]{2,1,0:T(8,128)(2,1)S(1)} collective-permute-done((bf16[1,104,128]{2,1,0:T(8,128)(2,1)S(1)}, bf16[1,104,128]{2,1,0:T(8,128)(2,1)S(1)}, u32[]{:S(2)}, u32[]{:S(2)}) %collective-permute-start.2) | collective-permute-done | bytes 26656 | tf_op jit(solution)/shard_map/ppermute | solution.py:778
  47.3 0.7 total.3.after_ref.refs_2_
  48.0 0.0 collective-permute-done.5.value_ref
  48.0 0.0 collective-permute-start.6
  48.0 0.5 collective-permute-start.4
  48.5 0.9 %collective-permute-start.3 = (bf16[2,1440,128]{2,1,0:T(8,128)(2,1)}, bf16[2,1440,128]{2,1,0:T(8,128)(2,1)S(1)}, u32[]{:S(2)}, u32[]{:S(2)}) collective-permute-start(bf16[2,1440,128]{2,1,0:T(8,128)(2,1)} %hold.4.own_ref), channel_id=1, source_target_pairs={{0,2},{2,0},{1,3},{3,1},{4,6},{6,4},{5,7},{7,5},{8,10},{10,8},{9,1... | collective-permute-start | bytes 2211848 | tf_op jit(solution)/shard_map/ppermute | solution.py:778
  49.5 3.4 %all-to-all-start.1 = ((bf16[8,104,128]{2,1,0:T(8,128)(2,1)}), bf16[8,104,128]{2,1,0:T(8,128)(2,1)S(1)}, u32[]{:S(2)}, u32[]{:S(2)}) async-start(bf16[8,104,128]{2,1,0:T(8,128)(2,1)} %total.3.after_ref.refs_2_), calls=%async_computation.1 | async-start | bytes 425984 | tf_op jit(solution)/shard_map/all_to_all | solution.py:782
  52.9 0.0 collective-permute-done.6.other_ref
  52.9 2.2 %widen.5 = (f32[2,180,32,128]{3,2,1,0:T(8,128)}, f32[2,180,32,128]{3,2,1,0:T(8,128)}, f32[8,128]{1,0:T(8,128)}) custom-call(s32[1]{0:T(128)} %bitcast.position_ref, bf16[2,1440,128]{2,1,0:T(8,128)(2,1)S(1)} %hold.5.own_ref, bf16[2,1440,128]{2,1,0:T(8,128)(2,1)S(1)} %collective-permute-done.6.other_ref, ...), custom_call_target="tpu_custom_call", output_to_operand_aliasing={{0}: (3, {}), {1}: (4, {})} | custom-call | tf_op jit(solution)/shard_map/widen/pallas_call | solution.py:807
  55.1 0.0 collective-permute-done.4.other_ref
  55.1 3.7 %widen.6 = (f32[2,180,32,128]{3,2,1,0:T(8,128)}, f32[2,180,32,128]{3,2,1,0:T(8,128)}, f32[8,128]{1,0:T(8,128)S(1)}) custom-call(s32[1]{0:T(128)} %bitcast.position_ref, bf16[2,1440,128]{2,1,0:T(8,128)(2,1)} %hold.4.own_ref, bf16[2,1440,128]{2,1,0:T(8,128)(2,1)S(1)} %collective-permute-done.4.other_ref, ...), custom_call_target="tpu_custom_call", output_to_operand_aliasing={{0}: (3, {}), {1}: (4, {})} | custom-call | tf_op jit(solution)/shard_map/widen/pallas_call | solution.py:807
  58.8 2.4 %all-to-all-done.1.value_ref = bf16[8,104,128]{2,1,0:T(8,128)(2,1)S(1)} async-done(((bf16[8,104,128]{2,1,0:T(8,128)(2,1)}), bf16[8,104,128]{2,1,0:T(8,128)(2,1)S(1)}, u32[]{:S(2)}, u32[]{:S(2)}) %all-to-all-start.1) | async-done | bytes 213024 | tf_op jit(solution)/shard_map/all_to_all | solution.py:782
  61.3 0.0 collective-permute-start.7
  61.3 6.0 %collective-permute-done.3.value_ref = bf16[2,1440,128]{2,1,0:T(8,128)(2,1)S(1)} collective-permute-done((bf16[2,1440,128]{2,1,0:T(8,128)(2,1)}, bf16[2,1440,128]{2,1,0:T(8,128)(2,1)S(1)}, u32[]{:S(2)}, u32[]{:S(2)}) %collective-permute-start.3) | collective-permute-done | bytes 737312 | tf_op jit(solution)/shard_map/ppermute | solution.py:778
  67.2 0.0 collective-permute-done.7.after_ref.other_ref
  67.2 0.0 collective-permute-start.8
  67.2 1.3 %unpack.1 = (f32[2,48,96]{2,1,0:T(8,128)}, f32[2,24,48]{2,1,0:T(8,128)}, f32[12,2,24]{2,1,0:T(2,128)}, f32[2,48,48]{2,1,0:T(8,128)}, f32[2,24,24]{2,1,0:T(8,128)...) custom-call(s32[1]{0:T(128)} %bitcast.position_ref, ...), custom_call_target="tpu_custom_call" | custom-call | tf_op jit(solution)/shard_map/unpack/pallas_call | solution.py:721
  68.5 1.0 %collective-permute-done.8.other_ref = bf16[2,1440,128]{2,1,0:T(8,128)(2,1)S(1)} collective-permute-done((bf16[2,1440,128]{2,1,0:T(8,128)(2,1)S(1)}, bf16[2,1440,128]{2,1,0:T(8,128)(2,1)S(1)}, u32[]{:S(2)}, u32[]{:S(2)}) %collective-permute-start.8) | collective-permute-done | bytes 737312 | tf_op jit(solution)/shard_map/ppermute | solution.py:778
  69.4 2.2 %widen.7 = (f32[2,180,32,128]{3,2,1,0:T(8,128)}, f32[2,180,32,128]{3,2,1,0:T(8,128)}, f32[8,128]{1,0:T(8,128)}) custom-call(s32[1]{0:T(128)} %bitcast.position_ref, bf16[2,1440,128]{2,1,0:T(8,128)(2,1)S(1)} %hold.7.own_ref, bf16[2,1440,128]{2,1,0:T(8,128)(2,1)S(1)} %collective-permute-done.8.other_ref, ...), custom_call_target="tpu_custom_call", output_to_operand_aliasing={{0}: (3, {}), {1}: (4, {})} | custom-call | tf_op jit(solution)/shard_map/widen/pallas_call | solution.py:807
  (5 shorter events, 0.0 us)
Async XLA Ops:
  22.6 12.3 %collective-permute-start.1 = (bf16[2,1440,128]{2,1,0:T(8,128)(2,1)}, bf16[2,1440,128]{2,1,0:T(8,128)(2,1)S(1)}, u32[]{:S(2)}, u32[]{:S(2)}) collective-permute-start(bf16[2,1440,128]{2,1,0:T(8,128)(2,1)} %get-tuple-element.59.own_ref), channel_id=1, source_target_pairs={{0,1},{1,0},{2,3},{3,2},{4,5},{5,4},{6,7},{7,6},{8,9},{9,8},{10,11... | collective-permute-start | bytes 2211848 | tf_op jit(solution)/shard_map/ppermute | solution.py:778
  23.1 24.9 %collective-permute-start.5 = (bf16[2,1440,128]{2,1,0:T(8,128)(2,1)}, bf16[2,1440,128]{2,1,0:T(8,128)(2,1)S(1)}, u32[]{:S(2)}, u32[]{:S(2)}) collective-permute-start(bf16[2,1440,128]{2,1,0:T(8,128)(2,1)} %get-tuple-element.59.own_ref), channel_id=1, source_target_pairs={{0,2},{2,0},{1,3},{3,1},{4,6},{6,4},{5,7},{7,5},{8,10},{10,8},{9,1... | collective-permute-start | bytes 2211848 | tf_op jit(solution)/shard_map/ppermute | solution.py:778
  25.7 1.7 %collective-permute-start = (bf16[832,128]{1,0:T(8,128)(2,1)}, bf16[832,128]{1,0:T(8,128)(2,1)S(1)}, u32[]{:S(2)}, u32[]{:S(2)}) collective-permute-start(bf16[832,128]{1,0:T(8,128)(2,1)} %get-tuple-element.58), channel_id=1, source_target_pairs={{0,1},{1,0},{2,3},{3,2},{4,5},{5,4},{6,7},{7,6},{8,9},{9,8},{10,11... | collective-permute-start | bytes 638984 | tf_op jit(solution)/shard_map/ppermute | solution.py:778
  27.4 0.9 %copy-start.1 = (bf16[832,128]{1,0:T(8,128)(2,1)S(1)}, bf16[832,128]{1,0:T(8,128)(2,1)}, u32[]{:S(2)}) copy-start(bf16[832,128]{1,0:T(8,128)(2,1)} %get-tuple-element.57.refs_0_) | copy-start | bytes 638980
  29.0 14.4 %all-to-all-start = ((bf16[8,104,128]{2,1,0:T(8,128)(2,1)}), bf16[8,104,128]{2,1,0:T(8,128)(2,1)S(1)}, u32[]{:S(2)}, u32[]{:S(2)}) async-start(bf16[8,104,128]{2,1,0:T(8,128)(2,1)} %join.1.refs_0_), calls=%async_computation | async-start | bytes 425984 | tf_op jit(solution)/shard_map/all_to_all | solution.py:782
  34.9 1.1 %copy-start = (bf16[2,1440,128]{2,1,0:T(8,128)(2,1)S(1)}, bf16[2,1440,128]{2,1,0:T(8,128)(2,1)}, u32[]{:S(2)}) copy-start(bf16[2,1440,128]{2,1,0:T(8,128)(2,1)} %get-tuple-element.59.own_ref) | copy-start | bytes 2211844
  43.4 3.9 %collective-permute-start.2 = (bf16[1,104,128]{2,1,0:T(8,128)(2,1)S(1)}, bf16[1,104,128]{2,1,0:T(8,128)(2,1)S(1)}, u32[]{:S(2)}, u32[]{:S(2)}) collective-permute-start(bf16[1,104,128]{2,1,0:T(8,128)(2,1)S(1)} %total.2.refs_0_), channel_id=1, source_target_pairs={{0,2},{2,0},{1,3},{3,1},{4,6},{6,4},{5,7},{7,5},{8,10},{10,8},{9,1... | collective-permute-start | bytes 79880 | tf_op jit(solution)/shard_map/ppermute | solution.py:778
  48.0 4.9 %collective-permute-start.6 = (bf16[2,1440,128]{2,1,0:T(8,128)(2,1)S(1)}, bf16[2,1440,128]{2,1,0:T(8,128)(2,1)S(1)}, u32[]{:S(2)}, u32[]{:S(2)}) collective-permute-start(bf16[2,1440,128]{2,1,0:T(8,128)(2,1)S(1)} %hold.5.own_ref), channel_id=1, source_target_pairs={{0,1},{1,0},{2,3},{3,2},{4,5},{5,4},{6,7},{7,6},{8,9},{9,8},{10,11... | collective-permute-start | bytes 2211848 | tf_op jit(solution)/shard_map/ppermute | solution.py:778
  48.0 7.1 %collective-permute-start.4 = (bf16[2,1440,128]{2,1,0:T(8,128)(2,1)}, bf16[2,1440,128]{2,1,0:T(8,128)(2,1)S(1)}, u32[]{:S(2)}, u32[]{:S(2)}) collective-permute-start(bf16[2,1440,128]{2,1,0:T(8,128)(2,1)} %hold.4.own_ref), channel_id=1, source_target_pairs={{0,1},{1,0},{2,3},{3,2},{4,5},{5,4},{6,7},{7,6},{8,9},{9,8},{10,11... | collective-permute-start | bytes 2211848 | tf_op jit(solution)/shard_map/ppermute | solution.py:778
  48.5 18.7 %collective-permute-start.3 = (bf16[2,1440,128]{2,1,0:T(8,128)(2,1)}, bf16[2,1440,128]{2,1,0:T(8,128)(2,1)S(1)}, u32[]{:S(2)}, u32[]{:S(2)}) collective-permute-start(bf16[2,1440,128]{2,1,0:T(8,128)(2,1)} %hold.4.own_ref), channel_id=1, source_target_pairs={{0,2},{2,0},{1,3},{3,1},{4,6},{6,4},{5,7},{7,5},{8,10},{10,8},{9,1... | collective-permute-start | bytes 2211848 | tf_op jit(solution)/shard_map/ppermute | solution.py:778
  49.5 11.8 %all-to-all-start.1 = ((bf16[8,104,128]{2,1,0:T(8,128)(2,1)}), bf16[8,104,128]{2,1,0:T(8,128)(2,1)S(1)}, u32[]{:S(2)}, u32[]{:S(2)}) async-start(bf16[8,104,128]{2,1,0:T(8,128)(2,1)} %total.3.after_ref.refs_2_), calls=%async_computation.1 | async-start | bytes 425984 | tf_op jit(solution)/shard_map/all_to_all | solution.py:782
  61.3 6.0 %collective-permute-start.7 = (bf16[8,104,128]{2,1,0:T(8,128)(2,1)S(1)}, bf16[8,104,128]{2,1,0:T(8,128)(2,1)S(1)}, u32[]{:S(2)}, u32[]{:S(2)}) collective-permute-start(bf16[8,104,128]{2,1,0:T(8,128)(2,1)S(1)} %hold.6.own_ref), channel_id=1, source_target_pairs={{0,1},{1,0},{2,3},{3,2},{4,5},{5,4},{6,7},{7,6},{8,9},{9,8},{10,11... | collective-permute-start | bytes 638984 | tf_op jit(solution)/shard_map/ppermute | solution.py:778
  67.2 2.2 %collective-permute-start.8 = (bf16[2,1440,128]{2,1,0:T(8,128)(2,1)S(1)}, bf16[2,1440,128]{2,1,0:T(8,128)(2,1)S(1)}, u32[]{:S(2)}, u32[]{:S(2)}) collective-permute-start(bf16[2,1440,128]{2,1,0:T(8,128)(2,1)S(1)} %hold.7.own_ref), channel_id=1, source_target_pairs={{0,1},{1,0},{2,3},{3,2},{4,5},{5,4},{6,7},{7,6},{8,9},{9,8},{10,11... | collective-permute-start | bytes 2211848 | tf_op jit(solution)/shard_map/ppermute | solution.py:778
